TPU v7x, 32 devices: a whole 2x2x4 slice. The times are simulated.
32 devices in a mesh: section: 4 (over y, x), batch: 8 (over z, core).
Axes of the slice: x: 2, y: 2, z: 4, core: 2. Of those that a mesh axis runs over, the one named last changes fastest.
Arguments:
- clean_mel: bfloat16 [16, 128, 80], P('batch'), may hold values from -6 to 6
- noise: bfloat16 [16, 128, 80], P('batch'), may hold values from -6 to 6
- phone_ids: int32 [16, 128], P('batch'), may hold values from 0 to 255
- segment_ids: int32 [16, 128], P('batch'), may hold values from 0 to 2, never falling along the last dimension, each value on 1 to 64 neighbouring positions
- loss_mask: int32 [16, 128], P('batch'), may hold values from 0 to 1, as said below
- time_idx: int32 [16], P('batch'), may hold values from 0 to 999
- attn_w: float32 [4, 2, 1024, 4096], P('section', None, 'batch')
- attn_m: float32 [4, 2, 1024, 4096], P('section', None, 'batch')
- attn_v: float32 [4, 2, 1024, 4096], P('section', None, 'batch'), as said below
- up_w: float32 [4, 2, 1024, 4096], P('section', None, 'batch'), may hold values from -0.1875 to 0.1875
- up_m: float32 [4, 2, 1024, 4096], P('section', None, 'batch')
- up_v: float32 [4, 2, 1024, 4096], P('section', None, 'batch'), as said below
- down_w: float32 [4, 2, 4096, 1024], P('section', None, 'batch'), may hold values from -0.09375 to 0.09375
- down_m: float32 [4, 2, 4096, 1024], P('section', None, 'batch')
- down_v: float32 [4, 2, 4096, 1024], P('section', None, 'batch'), as said below
- skip_w: float32 [4, 2048, 1024], P('section', 'batch'), may hold values from -0.125 to 0.125
- skip_m: float32 [4, 2048, 1024], P('section', 'batch')
- skip_v: float32 [4, 2048, 1024], P('section', 'batch'), as said below
- gain_w: float32 [4, 4, 1024], P('section', None, 'batch')
- gain_m: float32 [4, 4, 1024], P('section', None, 'batch')
- gain_v: float32 [4, 4, 1024], P('section', None, 'batch'), as said below
- table_w: float32 [497, 1024], replicated
- table_m: float32 [497, 1024], replicated
- table_v: float32 [497, 1024], replicated, as said below
Outputs:
- loss_sum: float32 [], replicated
- mask_total: float32 [], replicated
- grad_norm: float32 [], replicated
- attn_new: float32 [4, 2, 1024, 4096], P('section', None, 'batch')
- attn_first: float32 [4, 2, 1024, 4096], P('section', None, 'batch')
- attn_second: float32 [4, 2, 1024, 4096], P('section', None, 'batch')
- attn_copy: bfloat16 [4, 2, 1024, 4096], P('section', None, 'batch')
- up_new: float32 [4, 2, 1024, 4096], P('section', None, 'batch')
- up_first: float32 [4, 2, 1024, 4096], P('section', None, 'batch')
- up_second: float32 [4, 2, 1024, 4096], P('section', None, 'batch')
- up_copy: bfloat16 [4, 2, 1024, 4096], P('section', None, 'batch')
- down_new: float32 [4, 2, 4096, 1024], P('section', None, 'batch')
- down_first: float32 [4, 2, 4096, 1024], P('section', None, 'batch')
- down_second: float32 [4, 2, 4096, 1024], P('section', None, 'batch')
- down_copy: bfloat16 [4, 2, 4096, 1024], P('section', None, 'batch')
- skip_new: float32 [4, 2048, 1024], P('section', 'batch')
- skip_first: float32 [4, 2048, 1024], P('section', 'batch')
- skip_second: float32 [4, 2048, 1024], P('section', 'batch')
- skip_copy: bfloat16 [4, 2048, 1024], P('section', 'batch')
- gain_new: float32 [4, 4, 1024], P('section', None, 'batch')
- gain_first: float32 [4, 4, 1024], P('section', None, 'batch')
- gain_second: float32 [4, 4, 1024], P('section', None, 'batch')
- gain_copy: bfloat16 [4, 4, 1024], P('section', None, 'batch')
- table_new: float32 [497, 1024], replicated
- table_first: float32 [497, 1024], replicated
- table_second: float32 [497, 1024], replicated
- table_copy: bfloat16 [497, 1024], replicated
Inputs may be any that keep to these rules, and one draw needn't show every extreme that they name: `loss_mask`: in the first row a frame counts with probability one quarter, rising evenly to three quarters in the last row; the first frame of every row counts. `attn_v`: positive. `up_v`: positive. `down_v`: positive. `skip_v`: positive. `gain_v`: positive. `table_v`: positive.
All inputs are finite; a program needn't handle non-finite values.
Results may differ from a plain program's by a relative error of at most 0.012.
The roundings to bfloat16 on the way count: a program that leaves them out, or rounds other values in their place, can miss the bound.
Values may be sent and summed in bfloat16 or wider, within the bound.
No kernel may reach another device: no remote copies, remote signals or barrier semaphores. Data moves between devices by JAX's collectives and lax.ppermute only.
A program may use at most 576 MiB of HBM per device.

v0:
```python
from functools import partial
import math

import jax
import jax.numpy as jnp
from jax import lax
from jax.sharding import PartitionSpec as P

HEADS = 16
VOCAB = 256
TSTEPS = 1000
STEP = 10


norm_eps = 1e-05
beta_one = 0.9
beta_two = 0.999
adam_eps = 1e-08
rate_matrix = 0.02
rate_gain = 0.5
rate_table = 0.25
weight_decay = 0.01
clip_norm = 0.005
sigma_min = 1e-05


def passed_along(block, axis, distance):
    devices = range(lax.axis_size(axis))
    route = [(i - distance, i) for i in devices if i - distance in devices]
    return lax.ppermute(block, axis, route)


def to_low(operand):
    return operand.astype(jnp.bfloat16)


def matmul(left, right):
    return jnp.dot(left, right, preferred_element_type=jnp.float32)


def matmul_nt(left, right):
    return lax.dot_general(
        left, right, (((1,), (1,)), ((), ())), preferred_element_type=jnp.float32
    )


def matmul_tn(left, right):
    return lax.dot_general(
        left, right, (((0,), (0,)), ((), ())), preferred_element_type=jnp.float32
    )


def pick_row(array, slot_index):
    return lax.dynamic_index_in_dim(array, slot_index, 0, keepdims=False)


def store_row(buffer, slot_index, operand, is_live):
    merged = jnp.where(is_live, operand, pick_row(buffer, slot_index))
    return lax.dynamic_update_index_in_dim(buffer, merged, slot_index, 0)


def make_slots(count, tree):
    return jax.tree.map(lambda leaf: jnp.zeros((count,) + leaf.shape, leaf.dtype), tree)


def store_tree(buffers, slot_index, tree, is_live):
    return jax.tree.map(
        lambda buffer, leaf: store_row(buffer, slot_index, leaf, is_live), buffers, tree
    )


def pick_tree(buffers, slot_index):
    return jax.tree.map(lambda buffer: pick_row(buffer, slot_index), buffers)


def masked_run(is_live, function, operand):
    return lax.cond(
        is_live, function, lambda other: jax.tree.map(jnp.zeros_like, function(other)), operand
    )


def normalize(operand, gain):
    centered = operand - jnp.mean(operand, axis=-1, keepdims=True)
    return (
        centered
        * lax.rsqrt(jnp.mean(centered * centered, axis=-1, keepdims=True) + norm_eps)
        * gain
    )


def alibi_bias(row_len):
    position = jnp.arange(row_len, dtype=jnp.float32)
    slopes = 2.0 ** (-8.0 * jnp.arange(1, HEADS + 1, dtype=jnp.float32) / HEADS)
    return -slopes[:, None, None] * jnp.abs(position[:, None] - position[None, :])[None]


def frame_data(clean_mel, noise, phone_ids, loss_mask, time_idx, slot_index, model_dim):
    clean_rows = pick_row(clean_mel, slot_index).astype(jnp.float32)
    noise_rows = pick_row(noise, slot_index).astype(jnp.float32)
    weight = pick_row(loss_mask, slot_index).astype(jnp.float32)
    flow_time = pick_row(time_idx, slot_index).astype(jnp.float32) / TSTEPS
    noisy_mel = (1.0 - (1.0 - sigma_min) * flow_time) * noise_rows + flow_time * clean_rows
    context = clean_rows * (1.0 - weight)[:, None]
    target = clean_rows - (1.0 - sigma_min) * noise_rows
    mels = to_low(jnp.concatenate([noisy_mel, context], axis=1))
    onehot = (pick_row(phone_ids, slot_index)[:, None] == jnp.arange(VOCAB)[None, :]).astype(
        jnp.bfloat16
    )
    half_dim = model_dim // 2
    frequency = jnp.exp(-math.log(10000.0) * jnp.arange(half_dim, dtype=jnp.float32) / half_dim) * (
        1000.0 * flow_time
    )
    timing = jnp.concatenate([jnp.sin(frequency), jnp.cos(frequency)])
    return (mels, onehot, target, weight, timing)


def attention_parts(qkv, segments):
    row_len = qkv.shape[0]
    model_dim = qkv.shape[1] // 3
    head_size = model_dim // HEADS
    split_qkv = qkv.reshape(row_len, 3, HEADS, head_size)
    scores = jnp.einsum(
        "qhd,khd->hqk", split_qkv[:, 0], split_qkv[:, 1], preferred_element_type=jnp.float32
    ) * head_size ** (-0.5)
    scores = scores + alibi_bias(row_len)
    allowed = segments[:, None] == segments[None, :]
    scores = jnp.where(allowed[None], scores, -1e30)
    attn_probs = jax.nn.softmax(scores, axis=-1)
    probs_low = to_low(attn_probs)
    context = jnp.einsum(
        "hqk,khd->qhd", probs_low, split_qkv[:, 2], preferred_element_type=jnp.float32
    )
    return (split_qkv, attn_probs, probs_low, to_low(context.reshape(row_len, model_dim)))


def layer_forward(inputs, skip_in, weights, gains, segments):
    w_attn, w_up, w_down, w_skip = weights
    model_dim = inputs.shape[1]
    if w_skip is None:
        joined = inputs
        residual = inputs.astype(jnp.float32)
    else:
        joined = jnp.concatenate([inputs, skip_in], axis=1)
        residual = matmul(joined, w_skip)
    attn_in = to_low(normalize(residual, gains[0]))
    qkv = to_low(matmul(attn_in, w_attn[:, : 3 * model_dim]))
    split_qkv, attn_probs, probs_low, context = attention_parts(qkv, segments)
    middle = residual + matmul(context, w_attn[:, 3 * model_dim :])
    ffn_in = to_low(normalize(middle, gains[1]))
    hidden = matmul(ffn_in, w_up)
    active = to_low(jax.nn.gelu(hidden, approximate=False))
    output = middle + matmul(active, w_down)
    kept = (
        joined,
        residual,
        attn_in,
        split_qkv,
        attn_probs,
        probs_low,
        context,
        middle,
        ffn_in,
        hidden,
        active,
    )
    return (output, kept)


def layer_backward(grad_out, kept, weights, gains):
    w_attn, w_up, w_down, w_skip = weights
    row_len, model_dim = grad_out.shape
    head_size = model_dim // HEADS
    (
        joined,
        residual,
        attn_in,
        split_qkv,
        attn_probs,
        probs_low,
        context,
        middle,
        ffn_in,
        hidden,
        active,
    ) = kept
    branch_low = to_low(grad_out)
    d_down = matmul_tn(active, branch_low)
    _, gelu_back = jax.vjp(partial(jax.nn.gelu, approximate=False), hidden)
    hidden_low = to_low(gelu_back(matmul_nt(branch_low, w_down))[0])
    d_up = matmul_tn(ffn_in, hidden_low)
    _, norm_back = jax.vjp(normalize, middle, gains[1])
    d_middle, d_gain_ffn = norm_back(matmul_nt(hidden_low, w_up))
    d_middle = d_middle + grad_out
    proj_low = to_low(d_middle)
    d_proj = matmul_tn(context, proj_low)
    d_context = to_low(matmul_nt(proj_low, w_attn[:, 3 * model_dim :])).reshape(
        row_len, HEADS, head_size
    )
    d_probs = jnp.einsum(
        "qhd,khd->hqk", d_context, split_qkv[:, 2], preferred_element_type=jnp.float32
    )
    d_values = jnp.einsum("hqk,qhd->khd", probs_low, d_context, preferred_element_type=jnp.float32)
    d_scores = to_low(
        attn_probs * (d_probs - jnp.sum(d_probs * attn_probs, axis=-1, keepdims=True))
    )
    d_queries = jnp.einsum(
        "hqk,khd->qhd", d_scores, split_qkv[:, 1], preferred_element_type=jnp.float32
    ) * head_size ** (-0.5)
    d_key_part = jnp.einsum(
        "hqk,qhd->khd", d_scores, split_qkv[:, 0], preferred_element_type=jnp.float32
    ) * head_size ** (-0.5)
    qkv_low = to_low(
        jnp.stack([d_queries, d_key_part, d_values], axis=1).reshape(row_len, 3 * model_dim)
    )
    d_qkv = matmul_tn(attn_in, qkv_low)
    _, norm_back = jax.vjp(normalize, residual, gains[0])
    d_residual, d_gain_attn = norm_back(matmul_nt(qkv_low, w_attn[:, : 3 * model_dim]))
    d_residual = d_residual + d_middle
    d_gains = jnp.stack([d_gain_attn, d_gain_ffn])
    d_attn = jnp.concatenate([d_qkv, d_proj], axis=1)
    if w_skip is None:
        return (d_residual, None, (d_attn, d_up, d_down, None, d_gains))
    residual_low = to_low(d_residual)
    d_joined = matmul_nt(residual_low, w_skip)
    return (
        d_joined[:, :model_dim],
        d_joined[:, model_dim:],
        (d_attn, d_up, d_down, matmul_tn(joined, residual_low), d_gains),
    )


def head_pass(final_out, target, weight, head_rows, out_gain, mask_total):
    mel_bins = head_rows.shape[0]
    final_wide = final_out.astype(jnp.float32)
    normed = to_low(normalize(final_wide, out_gain))
    predicted = matmul_nt(normed, head_rows)
    error_mel = predicted - target
    loss_value = jnp.sum(weight * jnp.mean(error_mel * error_mel, axis=-1))
    d_pred = to_low(2.0 * error_mel * weight[:, None] / (mel_bins * mask_total))
    d_head = matmul_tn(d_pred, normed)
    _, norm_back = jax.vjp(normalize, final_wide, out_gain)
    d_final, d_gain = norm_back(matmul(d_pred, head_rows))
    return (loss_value, d_final, d_head, d_gain)


def adam_update(master, first, second, gradient, factor, step_rate):
    gradient = gradient * factor
    first_new = beta_one * first + (1.0 - beta_one) * gradient
    second_new = beta_two * second + (1.0 - beta_two) * gradient * gradient
    corrected = first_new / (1.0 - beta_one**STEP)
    spread = jnp.sqrt(second_new / (1.0 - beta_two**STEP))
    master_new = master - step_rate * (corrected / (spread + adam_eps) + weight_decay * master)
    return (master_new, first_new, second_new, master_new.astype(jnp.bfloat16))


def zeros_like_weights(weights):
    return jax.tree.map(lambda weight_arr: jnp.zeros(weight_arr.shape, jnp.float32), weights)


def body(
    clean_mel,
    noise,
    phone_ids,
    segment_ids,
    loss_mask,
    time_idx,
    attn_w,
    attn_m,
    attn_v,
    up_w,
    up_m,
    up_v,
    down_w,
    down_m,
    down_v,
    skip_w,
    skip_m,
    skip_v,
    gain_w,
    gain_m,
    gain_v,
    table_w,
    table_m,
    table_v,
):
    sections = lax.axis_size("section")
    section_id = lax.axis_index("section")
    micro_count, row_len, mel_bins = clean_mel.shape
    model_dim = attn_w.shape[3] // 4
    is_first = section_id == 0
    is_top = section_id == sections - 1
    tick_count = micro_count + sections - 1
    gathered = (
        lax.all_gather(to_low(attn_w), "batch", axis=2, tiled=True),
        lax.all_gather(to_low(up_w), "batch", axis=2, tiled=True),
        lax.all_gather(to_low(down_w), "batch", axis=2, tiled=True),
        lax.all_gather(to_low(skip_w), "batch", axis=1, tiled=True),
        lax.all_gather(to_low(gain_w), "batch", axis=2, tiled=True),
    )
    attn_all, up_all, down_all = (gathered[0][0], gathered[1][0], gathered[2][0])
    gain_all = gathered[4][0].astype(jnp.float32)
    encoder = (attn_all[0], up_all[0], down_all[0], None)
    decoder = (attn_all[1], up_all[1], down_all[1], gathered[3][0])
    front_table = to_low(table_w)
    mel_rows = front_table[: 2 * mel_bins]
    phone_rows = front_table[2 * mel_bins : 2 * mel_bins + VOCAB]
    head_rows = front_table[2 * mel_bins + VOCAB : 3 * mel_bins + VOCAB]
    out_gain = front_table[3 * mel_bins + VOCAB].astype(jnp.float32)
    mask_total = lax.psum(jnp.sum(loss_mask.astype(jnp.float32)), "batch")

    def inputs_of(slot_index):
        return frame_data(clean_mel, noise, phone_ids, loss_mask, time_idx, slot_index, model_dim)

    plane = jnp.zeros((micro_count, row_len, model_dim), jnp.bfloat16)
    enc_outputs, top_grads = (plane, plane)
    enc_kept = None
    arriving = jnp.zeros((row_len, model_dim), jnp.bfloat16)
    for tick_idx in range(tick_count):
        lag_count = tick_idx - section_id
        is_live = (lag_count >= 0) & (lag_count < micro_count)
        slot_index = jnp.clip(lag_count, 0, micro_count - 1)

        def run_encoder(operand):
            mels, onehot, target, weight, timing = inputs_of(slot_index)
            embedded = to_low(matmul(mels, mel_rows) + matmul(onehot, phone_rows) + timing[None])
            layer_input = jnp.where(is_first, embedded, operand)
            output, kept = layer_forward(
                layer_input, None, encoder, gain_all[0:2], pick_row(segment_ids, slot_index)
            )
            return (to_low(output), kept)

        leaving, kept = masked_run(is_live, run_encoder, arriving)
        if enc_kept is None:
            enc_kept = make_slots(micro_count, kept)
        enc_kept = store_tree(enc_kept, slot_index, kept, is_live)
        enc_outputs = store_row(enc_outputs, slot_index, leaving, is_live)
        if tick_idx < tick_count - 1:
            arriving = passed_along(leaving, "section", 1)
    head_grads = jnp.zeros((micro_count, row_len, model_dim), jnp.float32)
    loss_local = jnp.zeros((), jnp.float32)
    head_total = (
        jnp.zeros((mel_bins, model_dim), jnp.float32),
        jnp.zeros((model_dim,), jnp.float32),
    )
    dec_kept = None
    arriving = jnp.zeros((row_len, model_dim), jnp.bfloat16)
    for tick_idx in range(tick_count):
        lag_count = tick_idx - (sections - 1 - section_id)
        is_live = (lag_count >= 0) & (lag_count < micro_count)
        slot_index = jnp.clip(lag_count, 0, micro_count - 1)

        def run_decoder(operand):
            skip_in = pick_row(enc_outputs, slot_index)
            layer_input = jnp.where(is_top, skip_in, operand)
            output, kept = layer_forward(
                layer_input, skip_in, decoder, gain_all[2:4], pick_row(segment_ids, slot_index)
            )
            final_low = to_low(output)
            row_inputs = inputs_of(slot_index)
            head_out = masked_run(
                is_first,
                lambda final_out: head_pass(
                    final_out, row_inputs[2], row_inputs[3], head_rows, out_gain, mask_total
                ),
                final_low,
            )
            return (final_low, kept, head_out)

        leaving, kept, head_out = masked_run(is_live, run_decoder, arriving)
        if dec_kept is None:
            dec_kept = make_slots(micro_count, kept)
        dec_kept = store_tree(dec_kept, slot_index, kept, is_live)
        head_grads = store_row(head_grads, slot_index, head_out[1], is_live)
        loss_local = loss_local + head_out[0]
        head_total = (head_total[0] + head_out[2], head_total[1] + head_out[3])
        if tick_idx < tick_count - 1:
            arriving = passed_along(leaving, "section", -1)
    dec_total = zeros_like_weights(decoder + (gain_all[2:4],))
    skip_grads = jnp.zeros((micro_count, row_len, model_dim), jnp.float32)
    arriving = jnp.zeros((row_len, model_dim), jnp.bfloat16)
    for tick_idx in range(tick_count):
        lag_count = tick_idx - section_id
        is_live = (lag_count >= 0) & (lag_count < micro_count)
        slot_index = jnp.clip(lag_count, 0, micro_count - 1)

        def back_decoder(operand):
            incoming, totals = operand
            grad_out = jnp.where(
                is_first, pick_row(head_grads, slot_index), incoming.astype(jnp.float32)
            )
            d_input, d_skip, gradients = layer_backward(
                grad_out, pick_tree(dec_kept, slot_index), decoder, gain_all[2:4]
            )
            return (to_low(d_input), d_skip, jax.tree.map(jnp.add, totals, gradients))

        def spare_decoder(operand):
            incoming, totals = operand
            return (jnp.zeros_like(incoming), jnp.zeros(incoming.shape, jnp.float32), totals)

        sent_back, d_skip, dec_total = lax.cond(
            is_live, back_decoder, spare_decoder, (arriving, dec_total)
        )
        skip_grads = store_row(skip_grads, slot_index, d_skip, is_live)
        top_grads = store_row(top_grads, slot_index, sent_back, is_live)
        if tick_idx < tick_count - 1:
            arriving = passed_along(sent_back, "section", 1)
    enc_total = zeros_like_weights(encoder + (gain_all[0:2],))
    embed_total = (
        jnp.zeros((2 * mel_bins, model_dim), jnp.float32),
        jnp.zeros((VOCAB, model_dim), jnp.float32),
    )
    arriving = jnp.zeros((row_len, model_dim), jnp.bfloat16)
    for tick_idx in range(tick_count):
        lag_count = tick_idx - (sections - 1 - section_id)
        is_live = (lag_count >= 0) & (lag_count < micro_count)
        slot_index = jnp.clip(lag_count, 0, micro_count - 1)

        def back_encoder(operand):
            incoming, totals, embeds = operand
            grad_out = jnp.where(is_top, pick_row(top_grads, slot_index), incoming).astype(
                jnp.float32
            ) + pick_row(skip_grads, slot_index)
            d_input, _, gradients = layer_backward(
                grad_out, pick_tree(enc_kept, slot_index), encoder, gain_all[0:2]
            )
            sent_low = to_low(d_input)
            row_inputs = inputs_of(slot_index)
            embed_grads = masked_run(
                is_first,
                lambda grad_low: (
                    matmul_tn(row_inputs[0], grad_low),
                    matmul_tn(row_inputs[1], grad_low),
                ),
                sent_low,
            )
            return (
                sent_low,
                jax.tree.map(jnp.add, totals, gradients),
                (embeds[0] + embed_grads[0], embeds[1] + embed_grads[1]),
            )

        def spare_encoder(operand):
            incoming, totals, embeds = operand
            return (jnp.zeros_like(incoming), totals, embeds)

        sent_back, enc_total, embed_total = lax.cond(
            is_live, back_encoder, spare_encoder, (arriving, enc_total, embed_total)
        )
        if tick_idx < tick_count - 1:
            arriving = passed_along(sent_back, "section", -1)
    shards = (
        lax.psum_scatter(
            jnp.stack([enc_total[0], dec_total[0]])[None], "batch", scatter_dimension=2, tiled=True
        ),
        lax.psum_scatter(
            jnp.stack([enc_total[1], dec_total[1]])[None], "batch", scatter_dimension=2, tiled=True
        ),
        lax.psum_scatter(
            jnp.stack([enc_total[2], dec_total[2]])[None], "batch", scatter_dimension=2, tiled=True
        ),
        lax.psum_scatter(dec_total[3][None], "batch", scatter_dimension=1, tiled=True),
        lax.psum_scatter(
            jnp.concatenate([enc_total[4], dec_total[4]], axis=0)[None],
            "batch",
            scatter_dimension=2,
            tiled=True,
        ),
    )
    table_local = jnp.concatenate(
        [embed_total[0], embed_total[1], head_total[0], head_total[1][None]], axis=0
    )
    layer_squares = sum((jnp.sum(shard * shard) for shard in shards))
    table_grad, loss_sum, grand_squares = lax.psum(
        (table_local, loss_local, layer_squares), ("section", "batch")
    )
    grad_norm = jnp.sqrt(grand_squares + jnp.sum(table_grad * table_grad))
    factor = clip_norm / jnp.maximum(grad_norm, clip_norm)
    attn_out = adam_update(attn_w, attn_m, attn_v, shards[0], factor, rate_matrix)
    up_out = adam_update(up_w, up_m, up_v, shards[1], factor, rate_matrix)
    down_out = adam_update(down_w, down_m, down_v, shards[2], factor, rate_matrix)
    skip_out = adam_update(skip_w, skip_m, skip_v, shards[3], factor, rate_matrix)
    gain_out = adam_update(gain_w, gain_m, gain_v, shards[4], factor, rate_gain)
    table_out = adam_update(table_w, table_m, table_v, table_grad, factor, rate_table)
    return (
        loss_sum,
        mask_total,
        grad_norm,
        attn_out[0],
        attn_out[1],
        attn_out[2],
        attn_out[3],
        up_out[0],
        up_out[1],
        up_out[2],
        up_out[3],
        down_out[0],
        down_out[1],
        down_out[2],
        down_out[3],
        skip_out[0],
        skip_out[1],
        skip_out[2],
        skip_out[3],
        gain_out[0],
        gain_out[1],
        gain_out[2],
        gain_out[3],
        table_out[0],
        table_out[1],
        table_out[2],
        table_out[3],
    )


def solution(mesh):
    return jax.shard_map(
        body,
        mesh=mesh,
        in_specs=(
            P("batch", None, None),
            P("batch", None, None),
            P("batch", None),
            P("batch", None),
            P("batch", None),
            P("batch"),
            P("section", None, "batch", None),
            P("section", None, "batch", None),
            P("section", None, "batch", None),
            P("section", None, "batch", None),
            P("section", None, "batch", None),
            P("section", None, "batch", None),
            P("section", None, "batch", None),
            P("section", None, "batch", None),
            P("section", None, "batch", None),
            P("section", "batch", None),
            P("section", "batch", None),
            P("section", "batch", None),
            P("section", None, "batch"),
            P("section", None, "batch"),
            P("section", None, "batch"),
            P(),
            P(),
            P(),
        ),
        out_specs=(
            P(),
            P(),
            P(),
            P("section", None, "batch", None),
            P("section", None, "batch", None),
            P("section", None, "batch", None),
            P("section", None, "batch", None),
            P("section", None, "batch", None),
            P("section", None, "batch", None),
            P("section", None, "batch", None),
            P("section", None, "batch", None),
            P("section", None, "batch", None),
            P("section", None, "batch", None),
            P("section", None, "batch", None),
            P("section", None, "batch", None),
            P("section", "batch", None),
            P("section", "batch", None),
            P("section", "batch", None),
            P("section", "batch", None),
            P("section", None, "batch"),
            P("section", None, "batch"),
            P("section", None, "batch"),
            P("section", None, "batch"),
            P(),
            P(),
            P(),
            P(),
        ),
        check_vma=False,
    )
```

profile of v0, /device:TPU:0, one launch (start us, length us, event | category | flops | bytes accessed | tf_op | source)
XLA Modules:
  0.0 3452.8 jit_solution(14540872571169583820)
XLA Ops:
  23.3 19.4 psum.28
  54.3 111.1 %all-gather.5.cloned.1.call-done = bf16[1,2,1024,4096]{3,2,1,0:T(8,128)(2,1)} async-done(((bf16[1,2,128,4096]{3,2,1,0:T(8,128)(2,1)}), bf16[1,2,1024,4096]{3,2,1,0:T(8,128)(2,1)}) %all-gather.5.cloned.1.call-update) | async-done | bytes 16777232 | tf_op jit(solution)/shard_map/all_gather | solution.py:294
  178.2 138.7 %all-gather.7.cloned.1.call-done = bf16[1,2,1024,4096]{3,2,1,0:T(8,128)(2,1)} async-done(((bf16[1,2,128,4096]{3,2,1,0:T(8,128)(2,1)}), bf16[1,2,1024,4096]{3,2,1,0:T(8,128)(2,1)}) %all-gather.7.cloned.1.call-update) | async-done | bytes 16777232 | tf_op jit(solution)/shard_map/all_gather | solution.py:295
  329.8 138.6 %all-gather.9.cloned.1.call-done = bf16[1,2,4096,1024]{3,2,1,0:T(8,128)(2,1)} async-done(((bf16[1,2,512,1024]{3,2,1,0:T(8,128)(2,1)}), bf16[1,2,4096,1024]{3,2,1,0:T(8,128)(2,1)}) %all-gather.9.cloned.1.call-update) | async-done | bytes 16777232 | tf_op jit(solution)/shard_map/all_gather | solution.py:296
  480.5 38.2 %conditional.30 = (bf16[128,1024]{1,0:T(8,128)(2,1)}, f32[128,1024]{1,0:T(8,128)S(1)}, bf16[128,1024]{1,0:T(8,128)(2,1)}, bf16[128,3,16,64]{0,3,2,1:T(8,128)(2,1...) conditional(s32[]{:T(128)} %convert_element_type.1228, ...), branch_computations={%region_0.0_spmd, %region_1.8_spmd} | conditional | flops 3437480704 | bytes 78198736 | solution.py:77
  566.6 56.9 %conditional.31 = (bf16[128,1024]{1,0:T(8,128)(2,1)}, f32[128,1024]{1,0:T(8,128)}, bf16[128,1024]{1,0:T(8,128)(2,1)}, bf16[128,3,16,64]{0,3,2,1:T(8,128)(2,1)}, ...) conditional(s32[]{:T(128)} %convert_element_type.1236, ...), branch_computations={%region_8.9_spmd, %region_9.16_spmd} | conditional | flops 3437480704 | bytes 75315568 | solution.py:77
  678.2 24.2 collective-permute-start.2
  868.4 16.3 conditional.36
  919.4 17.3 conditional.37
  970.1 63.6 %collective-permute-done.6 = bf16[128,1024]{1,0:T(8,128)(2,1)} collective-permute-done((bf16[128,1024]{1,0:T(8,128)(2,1)}, bf16[128,1024]{1,0:T(8,128)(2,1)}, u32[]{:S(2)}, u32[]{:S(2)}) %collective-permute-start.6) | collective-permute-done | bytes 262176 | tf_op jit(solution)/shard_map/ppermute | solution.py:30
  1033.7 60.3 %conditional.38 = (bf16[128,1024]{1,0:T(8,128)(2,1)}, bf16[128,2048]{1,0:T(8,128)(2,1)}, f32[128,1024]{1,0:T(8,128)}, bf16[128,1024]{1,0:T(8,128)(2,1)}, bf16[12...) conditional(s32[]{:T(128)} %convert_element_type.1246, ...), branch_computations={%region_93.94_spmd, %region_94.110_spmd} | conditional | flops 3933916160 | bytes 117996600 | solution.py:77
  1145.7 53.4 %conditional.39 = (bf16[128,2048]{1,0:T(8,128)(2,1)}, f32[128,1024]{1,0:T(8,128)}, bf16[128,1024]{1,0:T(8,128)(2,1)}, bf16[128,3,16,64]{0,3,2,1:T(8,128)(2,1)}, ...) conditional(s32[]{:T(128)} %convert_element_type.1247, ...), branch_computations={%region_110.111_spmd, %region_111.127_spmd} | conditional | flops 3933916160 | bytes 118254632 | solution.py:77
  1226.1 64.9 %conditional.40 = (bf16[128,1024]{1,0:T(8,128)(2,1)S(1)}, f32[128,1024]{1,0:T(8,128)S(1)}, f32[1024,4096]{1,0:T(8,128)}, f32[1024,4096]{1,0:T(8,128)}, f32[4096,...) conditional(s32[]{:T(128)} %convert_element_type.1228, () %tuple.307, (s32[]{:T(128)}, ...), branch_computations={%region_128.129_spmd, %region_129.141_spmd} | conditional | flops 7701134336 | bytes 241007136 | solution.py:400
  1297.4 85.6 %conditional.41 = (bf16[128,1024]{1,0:T(8,128)(2,1)S(1)}, f32[128,1024]{1,0:T(8,128)}, f32[1024,4096]{1,0:T(8,128)}, f32[1024,4096]{1,0:T(8,128)}, f32[4096,1024...) conditional(s32[]{:T(128)} %convert_element_type.1236, (f32[1024,4096]{1,0:T(8,128)}, ...), branch_computations={%region_141.142_spmd, %region_142.154_spmd} | conditional | flops 7716209664 | bytes 294230496 | solution.py:400
  1327.4 14.0 convolution_add_fusion.16
  1398.8 83.6 %collective-permute-start.10 = (bf16[128,1024]{1,0:T(8,128)(2,1)}, bf16[128,1024]{1,0:T(8,128)(2,1)S(1)}, u32[]{:S(2)}, u32[]{:S(2)}) collective-permute-start(bf16[128,1024]{1,0:T(8,128)(2,1)} %copy-done.358), channel_id=1, source_target_pairs={{0,8},{8,16},{16,24},{1,9},{9,17},{17,25},{2,10},{10,18},{18,26},{... | collective-permute-start | bytes 786440 | tf_op jit(solution)/shard_map/ppermute | solution.py:30
  1510.8 30.3 conditional.45
  1542.4 87.8 %collective-permute-done.12 = bf16[128,1024]{1,0:T(8,128)(2,1)S(1)} collective-permute-done((bf16[128,1024]{1,0:T(8,128)(2,1)}, bf16[128,1024]{1,0:T(8,128)(2,1)S(1)}, u32[]{:S(2)}, u32[]{:S(2)}) %collective-permute-start.12) | collective-permute-done | bytes 262176 | tf_op jit(solution)/shard_map/ppermute | solution.py:30
  1649.8 291.7 %collective-permute-done.14 = bf16[128,1024]{1,0:T(8,128)(2,1)S(1)} collective-permute-done((bf16[128,1024]{1,0:T(8,128)(2,1)}, bf16[128,1024]{1,0:T(8,128)(2,1)S(1)}, u32[]{:S(2)}, u32[]{:S(2)}) %collective-permute-start.14) | collective-permute-done | bytes 262176 | tf_op jit(solution)/shard_map/ppermute | solution.py:30
  1941.5 90.0 %conditional.48 = (bf16[128,1024]{1,0:T(8,128)(2,1)}, f32[1024,4096]{1,0:T(8,128)}, f32[1024,4096]{1,0:T(8,128)}, f32[4096,1024]{1,0:T(8,128)}, f32[2,1024]{1,0:...) conditional(s32[]{:T(128)} %convert_element_type.1246, (f32[1024,4096]{1,0:T(8,128)}, ...), branch_computations={%region_238.239_spmd, %region_239.253_spmd} | conditional | flops 6750209024 | bytes 275234656 | solution.py:446
  1959.3 14.3 convolution_add_fusion.31
  2040.0 84.1 %conditional.49 = (f32[2,1024]{1,0:T(2,128)S(1)}, f32[160,1024]{1,0:T(8,128)}, f32[256,1024]{1,0:T(8,128)}, f32[1,1024,4096]{2,1,0:T(8,128)}, f32[1,1024,4096]{2,1,0:T(8,128)}, /*index=5*/f32[1,4096,1024]{2,1,0:T(8,128)}) conditional(s32[]{:T(128)} %convert_element_type.1247, (f32[2,1024]{1,0:T(2,128)S(1)}, f32[160,1024]{1,0:T(8,128)}, ...), branch_computations={%region_253.254_spmd, %region_254.268_spmd} | conditional | flops 6750210048 | bytes 258457232 | solution.py:446
  2057.9 14.3 add_bitcast_fusion
  2125.8 23.1 maximum_bitcast_fusion
  2149.0 23.2 maximum_bitcast_fusion.1
  2172.3 23.8 maximum_bitcast_fusion.2
  2202.9 39.8 %reduce-scatter.14.cloned.1.call-done = f32[1,256,1024]{2,1,0:T(8,128)} async-done(((f32[1,2048,1024]{2,1,0:T(8,128)}), f32[1,256,1024]{2,1,0:T(8,128)}) %reduce-scatter.14.cloned.1.call-update) | async-done | bytes 1048592 | tf_op jit(solution)/shard_map/reduce_scatter | solution.py:461
  2244.8 324.3 %reduce-scatter.8.cloned.1.call-done = f32[1,2,128,4096]{3,2,1,0:T(8,128)} async-done(((f32[1,2,1024,4096]{3,2,1,0:T(8,128)}), f32[1,2,128,4096]{3,2,1,0:T(8,128)}) %reduce-scatter.8.cloned.1.call-update) | async-done | bytes 4194320 | tf_op jit(solution)/shard_map/reduce_scatter | solution.py:452
  2573.0 322.4 %reduce-scatter.10.cloned.1.call-done = f32[1,2,128,4096]{3,2,1,0:T(8,128)} async-done(((f32[1,2,1024,4096]{3,2,1,0:T(8,128)}), f32[1,2,128,4096]{3,2,1,0:T(8,128)}) %reduce-scatter.10.cloned.1.call-update) | async-done | bytes 4194320 | tf_op jit(solution)/shard_map/reduce_scatter | solution.py:455
  2900.6 321.2 %reduce-scatter.12.cloned.1.call-done = f32[1,2,512,1024]{3,2,1,0:T(8,128)} async-done(((f32[1,2,4096,1024]{3,2,1,0:T(8,128)}), f32[1,2,512,1024]{3,2,1,0:T(8,128)}) %reduce-scatter.12.cloned.1.call-update) | async-done | bytes 4194320 | tf_op jit(solution)/shard_map/reduce_scatter | solution.py:458
  3227.7 131.8 %all-reduce.3.cloned.1.call-done = f32[497,1024]{1,0:T(8,128)} async-done(((f32[497,1024]{1,0:T(8,128)}), f32[497,1024]{1,0:T(8,128)}) %all-reduce.3.cloned.1.call-update) | async-done | bytes 2035728 | tf_op jit(solution)/shard_map/psum | solution.py:473
  3362.2 39.5 %all-reduce = (f32[]{:T(128)}, f32[]{:T(128)}) all-reduce(f32[]{:T(128)S(6)} %add.1556, f32[]{:T(128)S(6)} %add.1560), channel_id=1, replica_groups=mesh['section'=4,'batch'=8] {'section','batch'}, use_global_device_ids=true, to_apply=%region_127.128 | all-reduce | flops 2 | bytes 16 | tf_op jit(solution)/shard_map/psum | solution.py:473
  (1401 shorter events, 1228.3 us)
Async XLA Ops:
  7.2 158.2 %all-gather.5.cloned.1.call-start = ((), (), s32[]{:S(2)}) async-start(), calls=%async_computation.5 | async-start | bytes 18874368 | tf_op jit(solution)/shard_map/all_gather | solution.py:294
  11.1 305.8 %all-gather.7.cloned.1.call-start = ((), (), s32[]{:S(2)}) async-start(), calls=%async_computation.6 | async-start | bytes 18874368 | tf_op jit(solution)/shard_map/all_gather | solution.py:295
  14.9 453.5 %all-gather.9.cloned.1.call-start = ((), (), s32[]{:S(2)}) async-start(), calls=%async_computation.7 | async-start | bytes 18874368 | tf_op jit(solution)/shard_map/all_gather | solution.py:296
  18.9 794.9 %all-gather.11.cloned.1.call-start = ((), (), s32[]{:S(2)}) async-start(), calls=%async_computation.8 | async-start | bytes 4718592 | tf_op jit(solution)/shard_map/all_gather | solution.py:297
  20.9 2180.4 %reduce-scatter.16.cloned.1.call-start = ((), (), s32[]{:S(2)}) async-start(), calls=%async_computation.14 | async-start | bytes 589824
  22.6 457.9 %copy-start.81 = (bf16[256,1024]{1,0:T(8,128)(2,1)}, bf16[256,1024]{1,0:T(8,128)(2,1)S(1)}, u32[]{:S(2)}) copy-start(bf16[256,1024]{1,0:T(8,128)(2,1)S(1)} %slice.632) | copy-start | bytes 1572868
  329.8 150.7 %copy-start.246 = (bf16[2,128,80]{1,2,0:T(8,128)(2,1)S(1)}, bf16[2,128,80]{1,2,0:T(8,128)(2,1)}, u32[]{:S(2)}) copy-start(bf16[2,128,80]{1,2,0:T(8,128)(2,1)} %param.85) | copy-start | bytes 122884
  329.8 150.7 %copy-start.248 = (bf16[2,128,80]{1,2,0:T(8,128)(2,1)S(1)}, bf16[2,128,80]{1,2,0:T(8,128)(2,1)}, u32[]{:S(2)}) copy-start(bf16[2,128,80]{1,2,0:T(8,128)(2,1)} %param.84) | copy-start | bytes 122884
  518.7 47.9 %collective-permute-start = (bf16[128,1024]{1,0:T(8,128)(2,1)}, bf16[128,1024]{1,0:T(8,128)(2,1)}, u32[]{:S(2)}, u32[]{:S(2)}) collective-permute-start(bf16[128,1024]{1,0:T(8,128)(2,1)} %get-tuple-element.2121), channel_id=1, source_target_pairs={{0,8},{8,16},{16,24},{1,9},{9,17},{17,25},{2,10},{10,18},{18,26},{... | collective-permute-start | bytes 786440 | tf_op jit(solution)/shard_map/ppermute | solution.py:30
  623.5 44.0 %collective-permute-start.1 = (bf16[128,1024]{1,0:T(8,128)(2,1)}, bf16[128,1024]{1,0:T(8,128)(2,1)}, u32[]{:S(2)}, u32[]{:S(2)}) collective-permute-start(bf16[128,1024]{1,0:T(8,128)(2,1)} %get-tuple-element.2122), channel_id=1, source_target_pairs={{0,8},{8,16},{16,24},{1,9},{9,17},{17,25},{2,10},{10,18},{18,26},{... | collective-permute-start | bytes 786440 | tf_op jit(solution)/shard_map/ppermute | solution.py:30
  678.2 58.6 %collective-permute-start.2 = (bf16[128,1024]{1,0:T(8,128)(2,1)}, bf16[128,1024]{1,0:T(8,128)(2,1)}, u32[]{:S(2)}, u32[]{:S(2)}) collective-permute-start(bf16[128,1024]{1,0:T(8,128)(2,1)} %get-tuple-element.2123), channel_id=1, source_target_pairs={{0,8},{8,16},{16,24},{1,9},{9,17},{17,25},{2,10},{10,18},{18,26},{... | collective-permute-start | bytes 786440 | tf_op jit(solution)/shard_map/ppermute | solution.py:30
  752.1 43.8 %collective-permute-start.3 = (bf16[128,1024]{1,0:T(8,128)(2,1)}, bf16[128,1024]{1,0:T(8,128)(2,1)}, u32[]{:S(2)}, u32[]{:S(2)}) collective-permute-start(bf16[128,1024]{1,0:T(8,128)(2,1)} %get-tuple-element.2124), channel_id=1, source_target_pairs={{0,8},{8,16},{16,24},{1,9},{9,17},{17,25},{2,10},{10,18},{18,26},{... | collective-permute-start | bytes 786440 | tf_op jit(solution)/shard_map/ppermute | solution.py:30
  830.4 37.0 %collective-permute-start.4 = (bf16[128,1024]{1,0:T(8,128)(2,1)}, bf16[128,1024]{1,0:T(8,128)(2,1)}, u32[]{:S(2)}, u32[]{:S(2)}) collective-permute-start(bf16[128,1024]{1,0:T(8,128)(2,1)} %get-tuple-element.2127), channel_id=1, source_target_pairs={{8,0},{16,8},{24,16},{9,1},{17,9},{25,17},{10,2},{18,10},{26,18},{... | collective-permute-start | bytes 786440 | tf_op jit(solution)/shard_map/ppermute | solution.py:30
  894.9 24.5 collective-permute-start.5
  945.7 88.0 %collective-permute-start.6 = (bf16[128,1024]{1,0:T(8,128)(2,1)}, bf16[128,1024]{1,0:T(8,128)(2,1)}, u32[]{:S(2)}, u32[]{:S(2)}) collective-permute-start(bf16[128,1024]{1,0:T(8,128)(2,1)} %get-tuple-element.2131), channel_id=1, source_target_pairs={{8,0},{16,8},{24,16},{9,1},{17,9},{25,17},{10,2},{18,10},{26,18},{... | collective-permute-start | bytes 786440 | tf_op jit(solution)/shard_map/ppermute | solution.py:30
  1105.5 40.2 %collective-permute-start.7 = (bf16[128,1024]{1,0:T(8,128)(2,1)}, bf16[128,1024]{1,0:T(8,128)(2,1)}, u32[]{:S(2)}, u32[]{:S(2)}) collective-permute-start(bf16[128,1024]{1,0:T(8,128)(2,1)} %get-tuple-element.2133), channel_id=1, source_target_pairs={{8,0},{16,8},{24,16},{9,1},{17,9},{25,17},{10,2},{18,10},{26,18},{... | collective-permute-start | bytes 786440 | tf_op jit(solution)/shard_map/ppermute | solution.py:30
  1291.8 5.6 collective-permute-start.8
  1383.6 10.0 collective-permute-start.9
  1398.8 89.0 %collective-permute-start.10 = (bf16[128,1024]{1,0:T(8,128)(2,1)}, bf16[128,1024]{1,0:T(8,128)(2,1)S(1)}, u32[]{:S(2)}, u32[]{:S(2)}) collective-permute-start(bf16[128,1024]{1,0:T(8,128)(2,1)} %copy-done.358), channel_id=1, source_target_pairs={{0,8},{8,16},{16,24},{1,9},{9,17},{17,25},{2,10},{10,18},{18,26},{... | collective-permute-start | bytes 786440 | tf_op jit(solution)/shard_map/ppermute | solution.py:30
  1493.2 7.9 collective-permute-start.11
  1541.1 89.1 %collective-permute-start.12 = (bf16[128,1024]{1,0:T(8,128)(2,1)}, bf16[128,1024]{1,0:T(8,128)(2,1)S(1)}, u32[]{:S(2)}, u32[]{:S(2)}) collective-permute-start(bf16[128,1024]{1,0:T(8,128)(2,1)} %get-tuple-element.2281), channel_id=1, source_target_pairs={{8,0},{16,8},{24,16},{9,1},{17,9},{25,17},{10,2},{18,10},{26,18},{... | collective-permute-start | bytes 786440 | tf_op jit(solution)/shard_map/ppermute | solution.py:30
  1634.5 9.4 collective-permute-start.13
  1648.5 293.0 %collective-permute-start.14 = (bf16[128,1024]{1,0:T(8,128)(2,1)}, bf16[128,1024]{1,0:T(8,128)(2,1)S(1)}, u32[]{:S(2)}, u32[]{:S(2)}) collective-permute-start(bf16[128,1024]{1,0:T(8,128)(2,1)} %get-tuple-element.2295), channel_id=1, source_target_pairs={{8,0},{16,8},{24,16},{9,1},{17,9},{25,17},{10,2},{18,10},{26,18},{... | collective-permute-start | bytes 786440 | tf_op jit(solution)/shard_map/ppermute | solution.py:30
  2031.5 8.5 collective-permute-start.15
  2125.2 117.5 %reduce-scatter.14.cloned.1.call-start = ((), (), s32[]{:S(2)}) async-start(), calls=%async_computation.12 | async-start | bytes 9437184 | tf_op jit(solution)/shard_map/reduce_scatter | solution.py:461
  2125.8 443.3 %reduce-scatter.8.cloned.1.call-start = ((), (), s32[]{:S(2)}) async-start(), calls=%async_computation.9 | async-start | bytes 37748736 | tf_op jit(solution)/shard_map/reduce_scatter | solution.py:452
  2149.0 746.4 %reduce-scatter.10.cloned.1.call-start = ((), (), s32[]{:S(2)}) async-start(), calls=%async_computation.10 | async-start | bytes 37748736 | tf_op jit(solution)/shard_map/reduce_scatter | solution.py:455
  2172.2 1049.7 %reduce-scatter.12.cloned.1.call-start = ((), (), s32[]{:S(2)}) async-start(), calls=%async_computation.11 | async-start | bytes 37748736 | tf_op jit(solution)/shard_map/reduce_scatter | solution.py:458
  2196.1 1163.4 %all-reduce.3.cloned.1.call-start = ((), (), s32[]{:S(2)}) async-start(), calls=%async_computation.13 | async-start | bytes 4128768 | tf_op jit(solution)/shard_map/psum | solution.py:473
  2900.6 502.5 %copy-start.384 = (f32[1,4,128]{2,1,0:T(4,128)S(1)}, f32[1,4,128]{2,1,0:T(4,128)}, u32[]{:S(2)}) copy-start(f32[1,4,128]{2,1,0:T(4,128)} %param.102) | copy-start | bytes 6148
  2900.6 502.5 %copy-start.397 = (f32[1,4,128]{2,1,0:T(4,128)S(1)}, f32[1,4,128]{2,1,0:T(4,128)}, u32[]{:S(2)}) copy-start(f32[1,4,128]{2,1,0:T(4,128)} %param.103) | copy-start | bytes 6148
  2900.6 502.5 %copy-start.398 = (f32[1,4,128]{2,1,0:T(4,128)S(1)}, f32[1,4,128]{2,1,0:T(4,128)}, u32[]{:S(2)}) copy-start(f32[1,4,128]{2,1,0:T(4,128)} %param.104) | copy-start | bytes 6148
  (303 other events, 1574.4 us)
Sparse Core Ops, SparseCore 0:
  11.2 154.1 all-gather.4
  167.5 149.3 all-gather.6
  319.1 149.2 all-gather.8
  470.5 45.3 all-gather.10
  2125.3 27.3 reduce-scatter.15
  2154.9 87.7 reduce-scatter.13
  2245.2 323.8 reduce-scatter.7
  2571.5 323.8 reduce-scatter.9
  2897.9 323.8 reduce-scatter.11
  3227.6 131.7 all-reduce.2
where the time goes:
time: 3460 us; the launch traced here: 3450 us
  waiting for transfers between devices  1990 us (58%)
  local copies, waits for them, and re-layouts  440 us (13%)
  other arithmetic  398 us (12%)
  matrix products  342 us (10%)
  starting transfers between devices  144 us (4%)
  blocking collectives  69.9 us (2%)
  loops' own time  41.1 us (1%)
    ppermute x16, waiting for transfers between devices, passed_along(): return lax.ppermute(block, axis, route)  466 us
    reduce_scatter x1, waiting for transfers between devices, body(): lax.psum_scatter(jnp.stack([enc_total[0], dec_total[0]])[None], 'batch',...  324 us
    reduce_scatter x1, waiting for transfers between devices, body(): lax.psum_scatter(jnp.stack([enc_total[1], dec_total[1]])[None], 'batch',...  322 us
    reduce_scatter x1, waiting for transfers between devices, body(): lax.psum_scatter(jnp.stack([enc_total[2], dec_total[2]])[None], 'batch',...  321 us
    dynamic_slice x111, local copies, waits for them, and re-layouts, pick_row(): return lax.dynamic_index_in_dim(array, slot_index, 0, keepdims=False)  157 us
    ppermute x16, starting transfers between devices, passed_along(): return lax.ppermute(block, axis, route)  144 us
    all_gather x1, waiting for transfers between devices, body(): lax.all_gather(to_low(up_w), 'batch', axis=2, tiled=True)  139 us
    all_gather x1, waiting for transfers between devices, body(): lax.all_gather(to_low(down_w), 'batch', axis=2, tiled=True)  139 us
  transfers between devices with their start and end apart: 26, of which 15 were waited for; matrix products, arithmetic and copies ran while one was open for 16% of the time, Pallas kernels for 0%

commit v1 on v0

v1 whole, which is shorter than its diff:
```python
import math

import jax
import jax.numpy as jnp
from jax import lax
from jax.experimental import pallas as pl
from jax.experimental.pallas import tpu as pltpu
from jax.sharding import PartitionSpec as P

HEADS = 16
VOCAB = 256
TSTEPS = 1000
STEP = 10

norm_eps = 1e-05
beta_one = 0.9
beta_two = 0.999
adam_eps = 1e-08
rate_matrix = 0.02
rate_gain = 0.5
rate_table = 0.25
weight_decay = 0.01
clip_norm = 0.005
sigma_min = 1e-05

LAG = 2
BOTH = ("section", "batch")
BF16 = jnp.bfloat16
F32 = jnp.float32
BLOCK = 1024
SLOPES = [2.0 ** (-8.0 * (head + 1) / HEADS) for head in range(HEADS)]
VMEM_LIMIT = 16 * 2**20
QUICK = pl.CostEstimate(flops=1, bytes_accessed=1, transcendentals=0)


def to_low(operand):
    return operand.astype(BF16)


def matmul(left, right):
    return jnp.dot(left, right, preferred_element_type=F32)


def matmul_nt(left, right):
    return lax.dot_general(left, right, (((1,), (1,)), ((), ())), preferred_element_type=F32)


def matmul_tn(left, right):
    return lax.dot_general(left, right, (((0,), (0,)), ((), ())), preferred_element_type=F32)


def normalize(operand, gain):
    centered = operand - jnp.mean(operand, axis=-1, keepdims=True)
    variance = jnp.mean(centered * centered, axis=-1, keepdims=True)
    return centered * lax.rsqrt(variance + norm_eps) * gain


def normalize_back(grad, operand, gain):
    centered = operand - jnp.mean(operand, axis=-1, keepdims=True)
    scale = lax.rsqrt(jnp.mean(centered * centered, axis=-1, keepdims=True) + norm_eps)
    unit = centered * scale
    scaled = grad * gain
    along = jnp.mean(scaled * unit, axis=-1, keepdims=True)
    back = scale * (scaled - jnp.mean(scaled, axis=-1, keepdims=True) - unit * along)
    return back, jnp.sum(grad * unit, axis=0, keepdims=True)


def head_masks(rows):
    lanes = lax.broadcasted_iota(jnp.int32, (rows, 128), 1)
    return lanes < 64


def split_heads(slab, low_half):
    zero = jnp.zeros_like(slab)
    return jnp.concatenate(
        [jnp.where(low_half, slab, zero), jnp.where(low_half, zero, slab)], axis=0
    )


def live_slot(base, tick, steps_before):
    lag_count = tick - steps_before
    return (lag_count >= 0) & (lag_count < base[4]), jnp.clip(lag_count, 0, base[5] - 1)


def forward_kernel(
    base, tick_ref, arrived, embedded, skip_a, skip_b, skip_c, allowed, in_flight, gains,
    w_skip, w_attn, w_up, w_down,
    in_join, in_res, in_ain, in_qkv, in_prob, in_ctx, in_mid, in_fin, in_act, in_slope, in_final,
    leaving, o_join, o_res, o_ain, o_qkv, o_prob, o_ctx, o_mid, o_fin, o_act, o_slope, o_final,
    same_skip, same_attn, same_up, same_down,
    join, allow, res, ain, qkv, prob, ctx, mid, fin, act, slope, sent, acc, sem_in, sem_out,
):
    is_dec, pair, pos = base[0], base[1], base[2]
    is_live, slot = live_slot(base, tick_ref[0], LAG * pos + base[3])
    rows, width = res.shape
    hidden_size = act.shape[1]

    @pl.when(is_live)
    def _():
        first_half = join.at[:, pl.ds(0, width)]
        second_half = join.at[:, pl.ds(width, width)]
        from_rows = pltpu.make_async_copy(embedded.at[slot], first_half, sem_in.at[0])
        from_chain = pltpu.make_async_copy(arrived, first_half, sem_in.at[0])
        mask_copy = pltpu.make_async_copy(allowed.at[slot], allow, sem_in.at[2])
        skips = [
            pltpu.make_async_copy(source, second_half, sem_in.at[1])
            for source in (skip_a, skip_b, skip_c, arrived)
        ]

        @pl.when(pos == 0)
        def _():
            from_rows.start()

        @pl.when(pos != 0)
        def _():
            from_chain.start()

        @pl.when(is_dec == 1)
        def _():
            for which in range(4):

                @pl.when(pair == which)
                def _():
                    skips[which].start()

        mask_copy.start()
        from_chain.wait()
        outgoing = []

        def keep(source, target, index):
            copy = pltpu.make_async_copy(source, target.at[slot], sem_out.at[index])
            copy.start()
            outgoing.append(copy)

        @pl.when(is_dec == 1)
        def _():
            skips[0].wait()
            for start in range(0, width, BLOCK):
                cut = slice(start, start + BLOCK)
                res[:, cut] = matmul(join[...], w_skip[:, cut])

        @pl.when(is_dec == 0)
        def _():
            res[...] = join[:, :width].astype(F32)

        keep(join, o_join, 0)
        keep(res, o_res, 1)
        ain[...] = to_low(normalize(res[...], gains[0:1, :]))
        keep(ain, o_ain, 2)
        for start in range(0, 3 * width, BLOCK):
            cut = slice(start, start + BLOCK)
            qkv[:, cut] = to_low(matmul(ain[...], w_attn[:, cut]))
        keep(qkv, o_qkv, 3)
        mask_copy.wait()
        row_ids = lax.broadcasted_iota(jnp.int32, (rows, rows), 0)
        col_ids = lax.broadcasted_iota(jnp.int32, (rows, rows), 1)
        distance = jnp.abs(row_ids - col_ids).astype(F32)
        is_allowed = allow[...] > 0.5
        low_half = head_masks(rows)
        for two in range(HEADS // 2):
            cut = slice(two * 128, two * 128 + 128)
            queries = split_heads(qkv[:, cut], low_half)
            keys = qkv[:, width + two * 128 : width + two * 128 + 128]
            scores = matmul_nt(queries, keys) * 0.125
            prob[2 * two] = scores[:rows]
            prob[2 * two + 1] = scores[rows:]
        for head in range(HEADS):
            scores = jnp.where(is_allowed, prob[head] + (-SLOPES[head]) * distance, -1e30)
            powers = jnp.exp(scores - jnp.max(scores, axis=-1, keepdims=True))
            prob[head] = powers * (1.0 / jnp.sum(powers, axis=-1, keepdims=True))
        for two in range(HEADS // 2):
            cut = slice(two * 128, two * 128 + 128)
            values = qkv[:, 2 * width + two * 128 : 2 * width + two * 128 + 128]
            chances = jnp.concatenate([to_low(prob[2 * two]), to_low(prob[2 * two + 1])], axis=0)
            mixed = matmul(chances, values)
            ctx[:, cut] = to_low(jnp.where(low_half, mixed[:rows], mixed[rows:]))
        keep(prob, o_prob, 4)
        keep(ctx, o_ctx, 5)
        for start in range(0, width, BLOCK):
            cut = slice(start, start + BLOCK)
            column = 3 * width + start
            mid[:, cut] = res[:, cut] + matmul(ctx[...], w_attn[:, column : column + BLOCK])
        keep(mid, o_mid, 6)
        fin[...] = to_low(normalize(mid[...], gains[1:2, :]))
        keep(fin, o_fin, 7)
        for start in range(0, hidden_size, BLOCK):
            cut = slice(start, start + BLOCK)
            hidden = matmul(fin[...], w_up[:, cut])
            below = 0.5 + 0.5 * lax.erf(hidden * (2.0**-0.5))
            density = (2.0 * math.pi) ** -0.5 * jnp.exp(-0.5 * hidden * hidden)
            act[:, cut] = to_low(hidden * below)
            slope[:, cut] = to_low(below + hidden * density)
            part = matmul(act[:, cut], w_down[cut, :])
            if start == 0:
                acc[...] = part
            else:
                acc[...] += part
        keep(act, o_act, 8)
        keep(slope, o_slope, 9)
        sent[...] = to_low(mid[...] + acc[...])

        @pl.when(pos == base[6])
        def _():
            last = pltpu.make_async_copy(sent, o_final.at[slot], sem_in.at[1])
            last.start()
            last.wait()

        leave = pltpu.make_async_copy(sent, leaving, sem_in.at[0])
        leave.start()
        leave.wait()
        for copy in outgoing:
            copy.wait()


def backward_kernel(
    base, tick_ref, arrived, head_grads, skip_a, skip_b, skip_c, in_flight, gains,
    w_skip, w_attn, w_up, w_down, k_res, k_qkv, k_prob, k_mid, k_slope,
    in_branch, in_hid, in_proj, in_qkvg, in_resg, in_gain,
    leaving, leaving_skip, o_branch, o_hid, o_proj, o_qkvg, o_resg, o_gain,
    same_skip, same_attn, same_up, same_down,
    x_low, x_wide, x_skip, res, qkv, prob, mid, slope, grad, branch, hid, proj, qkvg, resg, gain_g,
    acc, ctx_g, joined, sem_in, sem_out,
):
    is_dec, pair, pos = base[0], base[1], base[2]
    is_live, slot = live_slot(base, tick_ref[0], LAG * (base[6] - pos))
    is_last = pos == base[6]
    rows, width = res.shape
    hidden_size = hid.shape[1]

    @pl.when(is_live)
    def _():
        from_head = pltpu.make_async_copy(head_grads.at[slot], x_wide, sem_in.at[0])
        from_chain = pltpu.make_async_copy(arrived, x_low, sem_in.at[1])
        skips = [
            pltpu.make_async_copy(source, x_skip, sem_in.at[2])
            for source in (skip_a, skip_b, skip_c)
        ]
        kept = [
            pltpu.make_async_copy(source.at[slot], target, sem_in.at[3 + index])
            for index, (source, target) in enumerate(
                ((k_slope, slope), (k_mid, mid), (k_prob, prob), (k_qkv, qkv), (k_res, res))
            )
        ]
        with_skip = (is_dec == 0) & (pair < 3)

        @pl.when(is_last)
        def _():
            from_head.start()

        @pl.when(jnp.logical_not(is_last))
        def _():
            from_chain.start()

        @pl.when(with_skip)
        def _():
            for which in range(3):

                @pl.when(pair == which)
                def _():
                    skips[which].start()

        for copy in kept:
            copy.start()
        outgoing = []

        def keep(source, target, index):
            copy = pltpu.make_async_copy(source, target.at[slot], sem_out.at[index])
            copy.start()
            outgoing.append(copy)

        @pl.when(is_last)
        def _():
            from_head.wait()
            grad[...] = x_wide[...]

        @pl.when(jnp.logical_not(is_last))
        def _():
            from_chain.wait()
            grad[...] = x_low[...].astype(F32)

        @pl.when(with_skip)
        def _():
            skips[0].wait()
            grad[...] += x_skip[...].astype(F32)

        branch[...] = to_low(grad[...])
        keep(branch, o_branch, 0)
        kept[0].wait()
        for start in range(0, hidden_size, BLOCK):
            cut = slice(start, start + BLOCK)
            hidden_low = to_low(matmul(branch[...], w_down[:, cut]) * slope[:, cut].astype(F32))
            hid[:, cut] = hidden_low
            part = matmul(hidden_low, w_up[cut, :])
            if start == 0:
                acc[...] = part
            else:
                acc[...] += part
        keep(hid, o_hid, 1)
        kept[1].wait()
        back, gain_back = normalize_back(acc[...], mid[...], gains[1:2, :])
        gain_g[1:2, :] = gain_back
        grad[...] += back
        proj[...] = to_low(grad[...])
        keep(proj, o_proj, 2)
        for start in range(0, width, BLOCK):
            cut = slice(start, start + BLOCK)
            ctx_g[:, cut] = to_low(matmul(proj[...], w_attn[3 * width :, cut]))
        kept[2].wait()
        kept[3].wait()
        low_half = head_masks(rows)
        for two in range(HEADS // 2):
            cut = slice(two * 128, two * 128 + 128)
            key_cut = slice(width + two * 128, width + two * 128 + 128)
            value_cut = slice(2 * width + two * 128, 2 * width + two * 128 + 128)
            outer_grad = split_heads(ctx_g[:, cut], low_half)
            prob_grad = matmul_nt(outer_grad, qkv[:, value_cut])
            chances = jnp.concatenate([prob[2 * two], prob[2 * two + 1]], axis=0)
            qkvg[:, value_cut] = to_low(matmul_tn(to_low(chances), outer_grad))
            total = jnp.sum(prob_grad * chances, axis=-1, keepdims=True)
            score_grad = to_low(chances * (prob_grad - total))
            query_grad = matmul(score_grad, qkv[:, key_cut]) * 0.125
            qkvg[:, cut] = to_low(jnp.where(low_half, query_grad[:rows], query_grad[rows:]))
            queries = split_heads(qkv[:, cut], low_half)
            qkvg[:, key_cut] = to_low(matmul_tn(score_grad, queries) * 0.125)
        keep(qkvg, o_qkvg, 3)
        for start in range(0, 3 * width, BLOCK):
            cut = slice(start, start + BLOCK)
            part = matmul(qkvg[:, cut], w_attn[cut, :])
            if start == 0:
                acc[...] = part
            else:
                acc[...] += part
        kept[4].wait()
        back, gain_back = normalize_back(acc[...], res[...], gains[0:1, :])
        gain_g[0:1, :] = gain_back
        gain_g[2:8, :] = jnp.zeros((6, width), F32)
        keep(gain_g, o_gain, 5)
        grad[...] += back
        resg[...] = to_low(grad[...])
        keep(resg, o_resg, 4)

        @pl.when(is_dec == 1)
        def _():
            for start in range(0, width, BLOCK):
                cut = slice(start, start + BLOCK)
                skip_cut = slice(width + start, width + start + BLOCK)
                input_grad = to_low(matmul(resg[...], w_skip[:, cut]))
                skip_grad = matmul(resg[...], w_skip[:, skip_cut])
                both = to_low(input_grad.astype(F32) + skip_grad)
                joined[:, cut] = jnp.where(pair == 3, both, input_grad)
                joined[:, skip_cut] = to_low(skip_grad)
            first = pltpu.make_async_copy(joined.at[:, pl.ds(0, width)], leaving, sem_in.at[0])
            second = pltpu.make_async_copy(
                joined.at[:, pl.ds(width, width)], leaving_skip, sem_in.at[1]
            )
            first.start()
            second.start()
            first.wait()
            second.wait()

        @pl.when(is_dec == 0)
        def _():
            first = pltpu.make_async_copy(resg, leaving, sem_in.at[0])
            first.start()
            first.wait()

        for copy in outgoing:
            copy.wait()


def kept_shapes(slots, rows, width, hidden_size):
    return [
        ((slots, rows, 2 * width), BF16),
        ((slots, rows, width), F32),
        ((slots, rows, width), BF16),
        ((slots, rows, 3 * width), BF16),
        ((slots, HEADS, rows, rows), F32),
        ((slots, rows, width), BF16),
        ((slots, rows, width), F32),
        ((slots, rows, width), BF16),
        ((slots, rows, hidden_size), BF16),
        ((slots, rows, hidden_size), BF16),
        ((slots, rows, width), BF16),
    ]


def grad_shapes(slots, rows, width, hidden_size):
    return [
        ((slots, rows, width), BF16),
        ((slots, rows, hidden_size), BF16),
        ((slots, rows, width), BF16),
        ((slots, rows, 3 * width), BF16),
        ((slots, rows, width), BF16),
        ((slots, 8, width), F32),
    ]


ANYWHERE = pl.BlockSpec(memory_space=pl.ANY)
IN_HBM = pl.BlockSpec(memory_space=pltpu.HBM)
IN_VMEM = pl.BlockSpec(memory_space=pltpu.VMEM)
IN_SMEM = pl.BlockSpec(memory_space=pltpu.SMEM)


def stay_in_hbm(array):
    return pltpu.with_memory_space_constraint(array, pltpu.HBM)


def all_ordered(arrays, earlier):
    count = len(arrays)
    return list(
        pl.pallas_call(
            lambda *refs: None,
            out_shape=[pltpu.HBM(array.shape, array.dtype) for array in arrays],
            in_specs=[IN_HBM] * (count + 1),
            out_specs=[IN_HBM] * count,
            input_output_aliases={index: index for index in range(count)},
            compiler_params=pltpu.CompilerParams(vmem_limit_bytes=2**20),
            cost_estimate=QUICK,
            name="ordered",
        )(*arrays, earlier)
    )


def ordered(array, earlier):
    return all_ordered([array], earlier)[0]


def same_in_vmem(arrays):
    return [pltpu.VMEM(array.shape, array.dtype) for array in arrays]


def unwritten(shapes):
    return list(
        pl.pallas_call(
            lambda *refs: None,
            out_shape=[pltpu.HBM(shape, dtype) for shape, dtype in shapes],
            out_specs=[IN_HBM] * len(shapes),
            compiler_params=pltpu.CompilerParams(vmem_limit_bytes=2**20),
            cost_estimate=QUICK,
            name="unwritten",
        )()
    )


def one_slot(shapes):
    return [pltpu.VMEM(shape[1:], dtype) for shape, dtype in shapes]


def forward_tick(base, tick, arrived, embedded, skips, allowed, in_flight, gains, weights, kept):
    slots, rows, width = embedded.shape
    hidden_size = weights[2].shape[1]
    shapes = kept_shapes(slots, rows, width, hidden_size)
    outputs = pl.pallas_call(
        forward_kernel,
        out_shape=[jax.ShapeDtypeStruct((rows, width), BF16)]
        + [pltpu.HBM(shape, dtype) for shape, dtype in shapes]
        + same_in_vmem(weights),
        in_specs=[IN_SMEM] * 2 + [ANYWHERE] * 7 + [IN_VMEM] * 5 + [IN_HBM] * 11,
        out_specs=[ANYWHERE] + [IN_HBM] * 11 + [IN_VMEM] * 4,
        input_output_aliases={14 + index: 1 + index for index in range(11)}
        | {10 + index: 12 + index for index in range(4)},
        scratch_shapes=one_slot(shapes[:1])
        + [pltpu.VMEM((rows, rows), F32)]
        + one_slot(shapes[1:])
        + [
            pltpu.VMEM((rows, width), F32),
            pltpu.SemaphoreType.DMA((3,)),
            pltpu.SemaphoreType.DMA((10,)),
        ],
        compiler_params=pltpu.CompilerParams(vmem_limit_bytes=VMEM_LIMIT),
        cost_estimate=QUICK,
        name="layer_forward",
    )(
        base,
        jnp.array([tick], jnp.int32),
        arrived,
        embedded,
        *skips,
        allowed,
        in_flight,
        gains,
        *weights,
        *kept,
    )
    return outputs[0], list(outputs[1:12]), list(outputs[12:])


def backward_tick(
    base, tick, arrived, head_grads, skips, in_flight, gains, weights, kept, grads
):
    slots, rows, width = head_grads.shape
    hidden_size = weights[2].shape[0]
    shapes = grad_shapes(slots, rows, width, hidden_size)
    was_kept = kept_shapes(slots, rows, width, hidden_size)
    read = [1, 3, 4, 6, 9]
    outputs = pl.pallas_call(
        backward_kernel,
        out_shape=[jax.ShapeDtypeStruct((rows, width), BF16)] * 2
        + [pltpu.HBM(shape, dtype) for shape, dtype in shapes]
        + same_in_vmem(weights),
        in_specs=[IN_SMEM] * 2 + [ANYWHERE] * 6 + [IN_VMEM] * 5 + [IN_HBM] * 11,
        out_specs=[ANYWHERE] * 2 + [IN_HBM] * 6 + [IN_VMEM] * 4,
        input_output_aliases={18 + index: 2 + index for index in range(6)}
        | {9 + index: 8 + index for index in range(4)},
        scratch_shapes=[
            pltpu.VMEM((rows, width), BF16),
            pltpu.VMEM((rows, width), F32),
            pltpu.VMEM((rows, width), BF16),
        ]
        + one_slot([was_kept[index] for index in read])
        + [pltpu.VMEM((rows, width), F32)]
        + one_slot(shapes)
        + [
            pltpu.VMEM((rows, width), F32),
            pltpu.VMEM((rows, width), BF16),
            pltpu.VMEM((rows, 2 * width), BF16),
            pltpu.SemaphoreType.DMA((8,)),
            pltpu.SemaphoreType.DMA((6,)),
        ],
        compiler_params=pltpu.CompilerParams(vmem_limit_bytes=VMEM_LIMIT),
        cost_estimate=QUICK,
        name="layer_backward",
    )(
        base,
        jnp.array([tick], jnp.int32),
        arrived,
        head_grads,
        *skips,
        in_flight,
        gains,
        *weights,
        *[stay_in_hbm(kept[index]) for index in read],
        *grads,
    )
    return outputs[0], outputs[1], list(outputs[2:8]), list(outputs[8:])


def transposed_shapes(weights):
    return [(weight.shape[::-1], BF16) for weight in weights]


def transpose_half(base, weight, target, half, for_dec):
    block = min(512, *weight.shape)

    def kernel(base_ref, source, start, same, out, stage, sems):
        @pl.when((base_ref[0] == (1 if for_dec else 0)) & (base_ref[7] == 0))
        def _():
            waiting = [None, None]
            steps = [
                (row, column)
                for row in range(0, source.shape[0], block)
                for column in range(0, source.shape[1], block)
            ]
            middle = len(steps) // 2
            steps = steps[middle:] if half else steps[:middle]
            for index, (row, column) in enumerate(steps):
                slot = index % 2
                if waiting[slot] is not None:
                    waiting[slot].wait()
                stage[slot] = source[row : row + block, column : column + block].T
                target = out.at[pl.ds(column, block), pl.ds(row, block)]
                waiting[slot] = pltpu.make_async_copy(stage.at[slot], target, sems.at[slot])
                waiting[slot].start()
            for copy in waiting:
                copy.wait()

    return pl.pallas_call(
        kernel,
        out_shape=[*same_in_vmem([weight]), pltpu.HBM(target.shape, target.dtype)],
        in_specs=[IN_SMEM, IN_VMEM, IN_HBM],
        out_specs=[IN_VMEM, IN_HBM],
        input_output_aliases={1: 0, 2: 1},
        scratch_shapes=[pltpu.VMEM((2, block, block), BF16), pltpu.SemaphoreType.DMA((2,))],
        compiler_params=pltpu.CompilerParams(vmem_limit_bytes=VMEM_LIMIT),
        cost_estimate=QUICK,
        name="transpose_half",
    )(base, weight, target)


def head_pass(
    base, final, target, frame_weight, head_rows, out_gain, scale, mel_bins, transposed
):
    slots, rows, width = final.shape
    count_weights = len(transposed)
    def kernel(
        base_ref, scale_ref, final_ref, target_ref, weight_ref, head_ref, gain_ref, *refs
    ):
        sources = refs[:count_weights]
        grads_ref, table_ref, gain_grad_ref, loss_ref = refs[count_weights : count_weights + 4]
        wholes = refs[count_weights + 4 : 2 * count_weights + 4]
        x_buf, out_buf, s_in, s_out, s_weights = refs[2 * count_weights + 4 :]
        moves = [
            pltpu.make_async_copy(source, whole, s_weights.at[index])
            for index, (source, whole) in enumerate(zip(sources, wholes))
        ]

        @pl.when(base_ref[7] == 0)
        def _():
            for move in moves:
                move.start()

        table_ref[...] = jnp.zeros((mel_bins, width), F32)
        gain_grad_ref[...] = jnp.zeros((1, width), F32)
        loss_ref[...] = jnp.zeros((rows, 128), F32)
        is_last = base_ref[2] == base_ref[6]
        count = base_ref[4]

        def row(i):
            load = pltpu.make_async_copy(final_ref.at[i], x_buf.at[i], s_in.at[i])
            load.wait()
            wide = x_buf[i].astype(F32)
            normed = to_low(normalize(wide, gain_ref[...]))
            error = matmul_nt(normed, head_ref[...]) - target_ref[i]
            weight = weight_ref[i]
            loss_ref[...] += weight * (error * error) * (1.0 / mel_bins)
            d_pred = to_low(error * weight * scale_ref[0])
            table_ref[...] += matmul_tn(d_pred, normed)[:mel_bins]
            back, gain_back = normalize_back(matmul(d_pred, head_ref[...]), wide, gain_ref[...])
            gain_grad_ref[...] += gain_back
            out_buf[i] = back
            pltpu.make_async_copy(out_buf.at[i], grads_ref.at[i], s_out.at[i]).start()

        @pl.when(is_last)
        def _():
            for i in range(slots):

                @pl.when(i < count)
                def _():
                    pltpu.make_async_copy(final_ref.at[i], x_buf.at[i], s_in.at[i]).start()

            for i in range(slots):
                pl.when(i < count)(lambda i=i: row(i))
            for i in range(slots):

                @pl.when(i < count)
                def _():
                    pltpu.make_async_copy(out_buf.at[i], grads_ref.at[i], s_out.at[i]).wait()

        @pl.when(base_ref[7] == 0)
        def _():
            for move in moves:
                move.wait()

    return pl.pallas_call(
        kernel,
        out_shape=[
            pltpu.HBM((slots, rows, width), F32),
            jax.ShapeDtypeStruct((mel_bins, width), F32),
            jax.ShapeDtypeStruct((1, width), F32),
            jax.ShapeDtypeStruct((rows, 128), F32),
        ]
        + same_in_vmem(transposed),
        in_specs=[IN_SMEM] * 2 + [IN_HBM] + [IN_VMEM] * 4 + [IN_HBM] * count_weights,
        out_specs=[IN_HBM] + [IN_VMEM] * (3 + count_weights),
        scratch_shapes=[
            pltpu.VMEM((slots, rows, width), BF16),
            pltpu.VMEM((slots, rows, width), F32),
            pltpu.SemaphoreType.DMA((slots,)),
            pltpu.SemaphoreType.DMA((slots,)),
            pltpu.SemaphoreType.DMA((count_weights,)),
        ],
        compiler_params=pltpu.CompilerParams(vmem_limit_bytes=VMEM_LIMIT),
        cost_estimate=QUICK,
        name="head_pass",
    )(base, scale, final, target, frame_weight, head_rows, out_gain, *transposed)


def table_pass(
    base, front, input_grads, gain_grads, head_total, out_gain_total, table_rows, earlier
):
    slots, rows, width = input_grads.shape
    front_rows, mel_bins = front.shape[1], head_total.shape[0]

    def kernel(
        base_ref, front_ref, grad_ref, gain_ref, earlier_ref, head_ref, out_ref, block_ref, x, y, g, sems
    ):
        is_dec = base_ref[0] == 1
        is_outer = base_ref[7] == 1
        block_ref[...] = jnp.zeros((table_rows + 16, width), BF16)
        tail = table_rows - front_rows - mel_bins
        block_ref[front_rows : front_rows + mel_bins, :] = to_low(head_ref[...])
        first = lax.broadcasted_iota(jnp.int32, (tail, width), 0) == 0
        block_ref[front_rows + mel_bins : table_rows, :] = to_low(
            jnp.where(first, out_ref[...], 0.0)
        )

        @pl.when(jnp.logical_not(is_outer))
        def _():
            load = pltpu.make_async_copy(gain_ref, g, sems.at[2])
            load.start()
            load.wait()
            total = g[0]
            for i in range(1, slots):
                total = total + g[i]
            own = jnp.concatenate([total, jnp.zeros((8, width), F32)], axis=0)
            moved = jnp.concatenate([jnp.zeros((2, width), F32), own[:14]], axis=0)
            block_ref[table_rows:, :] = to_low(jnp.where(is_dec, moved, own))

        @pl.when((base_ref[2] == 0) & jnp.logical_not(is_outer))
        def _():
            loads = [
                pltpu.make_async_copy(front_ref, x, sems.at[0]),
                pltpu.make_async_copy(grad_ref, y, sems.at[1]),
            ]
            for load in loads:
                load.start()
            for load in loads:
                load.wait()
            product = matmul_tn(x[...], y[...].reshape(slots * rows, width))
            block_ref[:front_rows, :] = to_low(product)

    return pl.pallas_call(
        kernel,
        out_shape=jax.ShapeDtypeStruct((table_rows + 16, width), BF16),
        in_specs=[IN_SMEM] + [IN_HBM] * 4 + [IN_VMEM] * 2,
        out_specs=IN_VMEM,
        scratch_shapes=[
            pltpu.VMEM(front.shape, BF16),
            pltpu.VMEM(input_grads.shape, BF16),
            pltpu.VMEM(gain_grads.shape, F32),
            pltpu.SemaphoreType.DMA((3,)),
        ],
        compiler_params=pltpu.CompilerParams(vmem_limit_bytes=VMEM_LIMIT),
        cost_estimate=QUICK,
        name="table_pass",
    )(
        base, stay_in_hbm(front), input_grads, gain_grads, stay_in_hbm(earlier), head_total,
        out_gain_total,
    )


def assemble(base, main_shards, skip_shards, span, width, hidden_size):
    main = [part for group in main_shards for part in group]
    skip = [part for group in skip_shards for part in group]
    sides = hidden_size // width
    per_main = 2 + sides

    def kernel(base_ref, *refs):
        main_refs, skip_refs = refs[: len(main)], refs[len(main) : len(main) + len(skip)]
        w_skip, w_attn, w_up, w_down, s_main, s_skip = refs[len(main) + len(skip) :]
        is_dec, quarter, rank = base_ref[0] == 1, base_ref[8], base_ref[9]
        which = [quarter, quarter ^ 1, jnp.where(is_dec, 1, 2), jnp.where(is_dec, 0, 3)]

        def rows_of(index, count):
            shard = which[index % 4] * span + (rank ^ (index // 4))
            return pl.multiple_of(shard * count, count)

        @pl.when(base_ref[7] == 0)
        def _():
            copies, skip_copies = [], []
            for index, source in enumerate(skip_refs):
                count = source.shape[0]
                target = w_skip.at[pl.ds(rows_of(index, count), count)]
                skip_copies.append(pltpu.make_async_copy(source, target, s_skip.at[index]))
            for index, source in enumerate(main_refs):
                count = source.shape[1]
                start = rows_of(index, count)
                sems = s_main.at[index]
                for place, whole in enumerate((w_attn, w_up)):
                    target = whole.at[pl.ds(start, count)]
                    copies.append(pltpu.make_async_copy(source.at[place], target, sems.at[place]))
                for side in range(sides):
                    block = source.at[2, :, pl.ds(side * width, width)]
                    row = pl.multiple_of(start * sides + side * count, count)
                    target = w_down.at[pl.ds(row, count)]
                    copies.append(pltpu.make_async_copy(block, target, sems.at[2 + side]))

            @pl.when(is_dec)
            def _():
                for copy in skip_copies:
                    copy.start()

            for copy in copies:
                copy.start()
            for copy in copies:
                copy.wait()

            @pl.when(is_dec)
            def _():
                for copy in skip_copies:
                    copy.wait()

    return list(
        pl.pallas_call(
            kernel,
            out_shape=[
                pltpu.VMEM((2 * width, width), BF16),
                pltpu.VMEM((width, 4 * width), BF16),
                pltpu.VMEM((width, hidden_size), BF16),
                pltpu.VMEM((hidden_size, width), BF16),
            ],
            in_specs=[IN_SMEM] + [IN_HBM] * (len(main) + len(skip)),
            out_specs=[IN_VMEM] * 4,
            scratch_shapes=[
                pltpu.SemaphoreType.DMA((len(main), per_main)),
                pltpu.SemaphoreType.DMA((len(skip),)),
            ],
            compiler_params=pltpu.CompilerParams(vmem_limit_bytes=VMEM_LIMIT),
            cost_estimate=QUICK,
            name="assemble",
        )(base, *(stay_in_hbm(part) for part in main + skip))
    )


def weight_products(base, first, slots_used, span, specs, lefts, rights, came, earlier):
    names_left, names_right = list(lefts), list(rights)
    direct = {name: lefts[name].ndim == 3 for name in names_left}
    units = []
    for matrix, (rows, cols, blocks) in enumerate(specs):
        quads = [tuple(range(4))] if 4 * rows <= 512 else [(q,) for q in range(4)]
        for left, right, source, column, size in blocks:
            for quad in quads:
                units.append((matrix, quad, rows, left, right, source, column, size))
    steps = [(other, unit) for other in (range(1, span) if first else (0,)) for unit in units]
    left_width = max(-(-len(quad) * rows // 128) * 128 for _, quad, rows, *_ in units)
    right_width = max(unit[7] for unit in units)
    side_cols = max(cols for _, cols, _ in specs)
    side_rows = min(rows for rows, _, _ in specs)
    outs = []
    if first:
        for rows, cols, _ in specs:
            outs += [pltpu.HBM((4, rows, cols), BF16)] * (span - 1)
    else:
        outs += [pltpu.HBM((len(specs), side_rows, side_cols), BF16)] * 3
        outs += [pltpu.HBM((rows, cols), F32) for rows, cols, _ in specs]
        outs += [pltpu.HBM((8, right_width), F32)]
    n_in = len(names_left) + len(names_right)
    n_came = len(came)

    def kernel(base_ref, *refs):
        left_refs = dict(zip(names_left, refs))
        right_refs = dict(zip(names_right, refs[len(names_left) :]))
        came_refs = refs[n_in : n_in + n_came]
        at = n_in + n_came + len(earlier)
        out_refs = refs[at : at + len(outs)]
        x_buf, y_buf, came_buf, low_buf, own_buf, sum_buf, s_x, s_y, s_came, s_out = refs[
            at + len(outs) :
        ]
        is_dec, rank = base_ref[0], base_ref[9]
        edge = jnp.where(is_dec == 1, 3, 0)
        own = jnp.where(is_dec == 1, 2, 1)
        near, far = jnp.where(is_dec == 1, 1, 2), jnp.where(is_dec == 1, 0, 3)

        def loads(index):
            other, (matrix, quad, rows, left, right, source, column, size) = steps[index]
            slot = index % 2
            copies = []
            for place, q in enumerate(quad):
                if direct[left]:
                    start = pl.multiple_of((q * span + (rank ^ other)) * rows, 128)
                    block = left_refs[left].at[pl.ds(0, slots_used), :, pl.ds(start, rows)]
                    target = x_buf.at[slot, :, :, pl.ds(place * rows, rows)]
                elif place == 0:
                    block = left_refs[left].at[rank ^ other, pl.ds(0, slots_used)]
                    target = x_buf.at[slot, :, :, pl.ds(0, lefts[left].shape[3])]
                else:
                    continue
                copies.append((block, target, s_x.at[slot, place]))
            block = right_refs[right].at[pl.ds(0, slots_used), :, pl.ds(source, size)]
            copies.append((block, y_buf.at[slot, :, :, pl.ds(0, size)], s_y.at[slot]))
            return [pltpu.make_async_copy(*copy) for copy in copies]

        def add_loads(index):
            _, (matrix, quad, rows, left, right, source, column, size) = steps[index]
            count = len(quad)
            copies = []
            for other in range(n_came // len(specs)):
                block = came_refs[matrix * (span - 1) + other].at[
                    pl.ds(quad[0], count), :, pl.ds(column, size)
                ]
                target = came_buf.at[other, pl.ds(0, count), pl.ds(0, rows), pl.ds(0, size)]
                copies.append(pltpu.make_async_copy(block, target, s_came.at[other]))
            return copies

        def run():
            for copy in loads(0):
                copy.start()
            sum_buf[...] = jnp.zeros(sum_buf.shape, F32)
            pending = {0: [], 1: []}
            for index, (other, unit) in enumerate(steps):
                matrix, quad, rows, left, right, source, column, size = unit
                slot, count = index % 2, len(quad)
                if index + 1 < len(steps):
                    for copy in loads(index + 1):
                        copy.start()
                adds = [] if first else add_loads(index)
                for copy in adds:
                    copy.start()
                for copy in loads(index):
                    copy.wait()
                deep = slots_used * x_buf.shape[2]
                x = x_buf[slot, :, :, : count * rows].reshape(deep, count * rows)
                y = y_buf[slot, :, :, :size].reshape(deep, size)
                total = matmul_tn(x, y).reshape(count, rows, size)
                for copy in adds:
                    copy.wait()
                for which in range(len(adds)):
                    total = total + came_buf[which, :count, :rows, :size].astype(F32)
                for copy in pending[slot]:
                    copy()
                pending[slot] = []
                low_buf[slot, :count, :rows, :size] = to_low(total)

                def send(block, target, sem, condition=None):
                    copy = pltpu.make_async_copy(block, target, sem)
                    if condition is None:
                        copy.start()
                        pending[slot].append(copy.wait)
                        return

                    @pl.when(condition)
                    def _():
                        copy.start()

                    def wait():
                        @pl.when(condition)
                        def _():
                            copy.wait()

                    pending[slot].append(wait)

                staged = low_buf.at[slot, :, pl.ds(0, rows), pl.ds(0, size)]
                wide = own_buf.at[slot, pl.ds(0, rows), pl.ds(0, size)]
                cut = pl.ds(column, size)
                if first:
                    send(
                        staged.at[pl.ds(0, count)],
                        out_refs[matrix * (span - 1) + other - 1].at[pl.ds(quad[0], count), :, cut],
                        s_out.at[slot, 0, 0],
                    )
                    continue
                parts = rows // side_rows
                for place, whose in enumerate((edge, near, far)):
                    for part in range(parts):
                        target = out_refs[place].at[
                            matrix, :, pl.ds(part * side_cols // parts + column, size)
                        ]
                        source = staged.at[
                            whose if count == 4 else 0, pl.ds(part * side_rows, side_rows)
                        ]
                        condition = None if count == 4 else whose == quad[0]
                        send(source, target, s_out.at[slot, place, part], condition)
                for place, q in enumerate(quad):

                    @pl.when(own == q)
                    def _():
                        own_buf[slot, :rows, :size] = total[place]
                        squares = (total[place] * total[place]).reshape(-1, 8, size)
                        sum_buf[:, :size] += jnp.sum(squares, axis=0)

                condition = None if count == 4 else own == quad[0]
                send(wide, out_refs[3 + matrix].at[:, cut], s_out.at[slot, 3, 0], condition)
            for slot in (0, 1):
                for copy in pending[slot]:
                    copy()
            if not first:
                copy = pltpu.make_async_copy(sum_buf, out_refs[-1], s_y.at[0])
                copy.start()
                copy.wait()

        pl.when(base_ref[7] == 0)(run)

    row_len = rights[names_right[0]].shape[1]
    tall = max(rows for rows, _, _ in specs)
    quad_rows = max(len(quad) for _, quad, *_ in units)
    results = pl.pallas_call(
        kernel,
        out_shape=outs,
        in_specs=[IN_SMEM] + [IN_HBM] * (n_in + n_came + len(earlier)),
        out_specs=[IN_HBM] * len(outs),
        scratch_shapes=[
            pltpu.VMEM((2, slots_used, row_len, left_width), BF16),
            pltpu.VMEM((2, slots_used, row_len, right_width), BF16),
            pltpu.VMEM((max(n_came // len(specs), 1), quad_rows, tall, right_width), BF16),
            pltpu.VMEM((2, quad_rows, tall, right_width), BF16),
            pltpu.VMEM((2, tall, right_width), F32),
            pltpu.VMEM((8, right_width), F32),
            pltpu.SemaphoreType.DMA((2, 4)),
            pltpu.SemaphoreType.DMA((2,)),
            pltpu.SemaphoreType.DMA((max(span - 1, 1),)),
            pltpu.SemaphoreType.DMA((2, 4, tall // side_rows)),
        ],
        compiler_params=pltpu.CompilerParams(vmem_limit_bytes=2 * VMEM_LIMIT),
        cost_estimate=QUICK,
        name="weight_products",
    )(base, *(stay_in_hbm(a) for a in (*lefts.values(), *rights.values(), *came, *earlier)))
    return list(results)


def adam_update(master, first, second, gradient, factor, step_rate):
    gradient = gradient * factor
    first_new = beta_one * first + (1.0 - beta_one) * gradient
    second_new = beta_two * second + (1.0 - beta_two) * gradient * gradient
    corrected = first_new / (1.0 - beta_one**STEP)
    spread = jnp.sqrt(second_new / (1.0 - beta_two**STEP))
    master_new = master - step_rate * (corrected / (spread + adam_eps) + weight_decay * master)
    return (master_new, first_new, second_new, master_new.astype(BF16))


def body(
    clean_mel,
    noise,
    phone_ids,
    segment_ids,
    loss_mask,
    time_idx,
    attn_w,
    attn_m,
    attn_v,
    up_w,
    up_m,
    up_v,
    down_w,
    down_m,
    down_v,
    skip_w,
    skip_m,
    skip_v,
    gain_w,
    gain_m,
    gain_v,
    table_w,
    table_m,
    table_v,
):
    sections = lax.axis_size("section")
    batch = lax.axis_size("batch")
    section_id = lax.axis_index("section")
    batch_id = lax.axis_index("batch")
    span = batch // 4
    quarter, rank = batch_id // span, batch_id % span
    is_dec = quarter >= 2
    is_outer = (quarter == 0) | (quarter == 3)
    local_rows, row_len, mel_bins = clean_mel.shape
    width = attn_w.shape[3] // 4
    hidden_size = up_w.shape[3]
    total_rows = local_rows * batch
    slots = total_rows // span
    top = 2 * sections - 1
    pos = jnp.where(is_dec, top - section_id, section_id)
    chain_rows = jnp.where(is_outer, 0, slots)
    base = jnp.stack(
        [is_dec, section_id, pos, 0, chain_rows, slots, top, is_outer, quarter, rank]
    ).astype(jnp.int32)

    near, far, back_far = ((1, 2), (2, 1)), ((0, 2), (3, 1)), ((1, 3), (2, 0))
    inward, outward = ((0, 1), (3, 2)), ((1, 0), (2, 3))

    def along(block, pairs):
        route = [(a * span + i, b * span + i) for a, b in pairs for i in range(span)]
        return lax.ppermute(block, "batch", route)

    def across(block, bits, members=(0, 1, 2, 3)):
        route = [(a * span + i, a * span + (i ^ bits)) for a in members for i in range(span)]
        return lax.ppermute(block, "batch", route)

    def flipped(block, axis, bit):
        return lax.ppermute(block, axis, [(i, i ^ bit) for i in range(lax.axis_size(axis))])

    def at_stage(stage):
        return (stage, 1) if stage < sections else (top - stage, 2)

    def stage_route(pairs):
        route = []
        for source, target in pairs:
            (s, a), (t, b) = at_stage(source), at_stage(target)
            route += [(s * batch + a * span + i, t * batch + b * span + i) for i in range(span)]
        return route

    chain_forward = stage_route([(stage, stage + 1) for stage in range(top)])
    chain_backward = stage_route([(stage + 1, stage) for stage in range(top)])
    skip_forward = stage_route([(s, top - s) for s in range(sections - 1)])
    skip_backward = stage_route([(top - s, s) for s in range(sections - 1)])

    times = jnp.stack([time_idx // 32, time_idx % 32], axis=1)
    small = [
        clean_mel.reshape(-1),
        noise.reshape(-1),
        to_low(jnp.stack([phone_ids, segment_ids, loss_mask], axis=1)).reshape(-1),
        to_low(times).reshape(-1),
        to_low(gain_w[0]).reshape(-1),
    ]
    sizes = [part.size for part in small]
    packed = jnp.pad(jnp.concatenate(small), (0, -sum(sizes) % 1024)).reshape(1, -1, 128)
    everyone = lax.all_gather(packed, "batch", axis=0, tiled=True).reshape(batch, -1)
    parts = []
    offset = 0
    for size in sizes:
        parts.append(everyone[:, offset : offset + size])
        offset += size

    def every_rank(piece, members):
        return [piece] + [across(piece, bits, members) for bits in range(1, span)]

    def gather_shards(enc_part, dec_part, only_dec):
        limit = (lambda pairs: tuple(p for p in pairs if p[1] >= 2)) if only_dec else (lambda p: p)
        members = (2,) if only_dec else (1, 2)
        own = ordered(jnp.where(is_dec, dec_part, enc_part), everyone)
        other = ordered(jnp.where(is_dec, enc_part, dec_part), everyone)
        pieces = (
            own,
            along(own, limit(inward)),
            along(other, limit(near)),
            along(other, limit(far)),
        )
        return [list(group) for group in zip(*(every_rank(p, members) for p in pieces))]

    def packed_shard(layer):
        rows = width // batch
        down = to_low(down_w[0, layer])
        side = [down[i * rows : (i + 1) * rows] for i in range(hidden_size // width)]
        return jnp.stack(
            [to_low(attn_w[0, layer]), to_low(up_w[0, layer]), jnp.concatenate(side, axis=1)]
        )

    skip_low = to_low(skip_w[0])
    skip_shards = gather_shards(skip_low, skip_low, True)
    main_shards = gather_shards(packed_shard(0), packed_shard(1), False)
    weights = assemble(base, main_shards, skip_shards, span, width, hidden_size)

    all_clean = parts[0].reshape(total_rows, row_len, mel_bins)
    all_noise = parts[1].reshape(total_rows, row_len, mel_bins)
    all_ids = parts[2].reshape(total_rows, 3, row_len).astype(F32)
    all_times = parts[3].reshape(total_rows, 2).astype(F32)
    all_gains = parts[4].reshape(batch, 4, width // batch)
    all_gains = jnp.moveaxis(all_gains, 0, 1).reshape(4, width).astype(F32)
    gains = jnp.where(is_dec, all_gains[2:4], all_gains[0:2])
    mask_total = jnp.sum(all_ids[:, 2])

    def chain_part(array):
        return lax.dynamic_slice_in_dim(array, rank * slots, slots, 0)

    clean_rows = chain_part(all_clean).astype(F32)
    noise_rows = chain_part(all_noise).astype(F32)
    ids = chain_part(all_ids)
    time_parts = chain_part(all_times)
    phones, segments, weight = ids[:, 0], ids[:, 1], ids[:, 2]
    flow_time = (time_parts[:, 0] * 32.0 + time_parts[:, 1]) / TSTEPS
    wide_time = flow_time[:, None, None]
    noisy_mel = (1.0 - (1.0 - sigma_min) * wide_time) * noise_rows + wide_time * clean_rows
    context_mel = clean_rows * (1.0 - weight)[..., None]
    target = clean_rows - (1.0 - sigma_min) * noise_rows
    onehot = to_low(phones[..., None] == jnp.arange(VOCAB, dtype=F32))
    front = jnp.concatenate([to_low(noisy_mel), to_low(context_mel), onehot], axis=2)
    half = width // 2
    frequency = jnp.exp(-math.log(10000.0) * jnp.arange(half, dtype=F32) / half) * (
        1000.0 * flow_time[:, None]
    )
    timing = jnp.concatenate([jnp.sin(frequency), jnp.cos(frequency)], axis=1)
    table_low = to_low(table_w)
    front_rows = 2 * mel_bins + VOCAB
    head_rows = table_low[front_rows : front_rows + mel_bins]
    out_gain = table_low[front_rows + mel_bins].astype(F32)[None]
    flat_front = front.reshape(slots * row_len, front_rows)
    embedded = (
        matmul(flat_front[:, : 2 * mel_bins], table_low[: 2 * mel_bins])
        + matmul(flat_front[:, 2 * mel_bins :], table_low[2 * mel_bins : front_rows])
    ).reshape(slots, row_len, width)
    embedded = to_low(embedded + timing[:, None, :])
    allowed = (segments[:, :, None] == segments[:, None, :]).astype(F32)
    frame_weight = jnp.broadcast_to(weight[..., None], (slots, row_len, 128))
    target = jnp.pad(target, ((0, 0), (0, 0), (0, 128 - mel_bins)))
    head_rows = jnp.pad(head_rows, ((0, 128 - mel_bins), (0, 0)))
    scale = (2.0 / (mel_bins * mask_total))[None]
    base, embedded, allowed, frame_weight, target, head_rows, out_gain, scale, flat_front = (
        lax.optimization_barrier(
            (base, embedded, allowed, frame_weight, target, head_rows, out_gain, scale, flat_front)
        )
    )
    embedded, allowed = stay_in_hbm(embedded), stay_in_hbm(allowed)

    kept = unwritten(kept_shapes(slots, row_len, width, hidden_size))
    transposed = unwritten(transposed_shapes(weights))
    blank = jnp.zeros((row_len, width), BF16)
    waits = [LAG * (top - 2 * s) for s in range(sections - 1)]
    soon = 2 * LAG
    tick_count = LAG * top + slots
    skip_sent, arriving = [], []
    for tick in range(tick_count):
        arrived = arriving[tick - LAG] if tick >= LAG else blank
        skips = [skip_sent[tick - wait] if tick >= wait else blank for wait in waits]
        in_flight = skip_sent[tick - soon] if tick >= soon else blank
        for for_dec, begin in ((True, 0), (False, LAG * (sections - 1) + slots - 2)):
            which, half = (tick - begin) // 2, (tick - begin) % 2
            if tick in range(begin, begin + 2 * len(weights)) and (for_dec or which):
                weights[which], transposed[which] = transpose_half(
                    base, weights[which], transposed[which], half, for_dec
                )
        output, kept, weights = forward_tick(
            base, tick, arrived, embedded, skips, allowed, in_flight, gains, weights, kept
        )
        arriving.append(lax.ppermute(output, BOTH, chain_forward))
        is_needed = tick < LAG * (sections - 2) + slots
        skip_sent.append(lax.ppermute(output, BOTH, skip_forward) if is_needed else blank)

    head_grads, head_total, out_gain_total, loss_parts, *weights = head_pass(
        base, kept[10], target, frame_weight, head_rows, out_gain, scale, mel_bins, transposed
    )

    head_grads = stay_in_hbm(head_grads)

    grads = unwritten(grad_shapes(slots, row_len, width, hidden_size))
    skip_sent, arriving = [], []
    for tick in range(tick_count):
        arrived = arriving[tick - LAG] if tick >= LAG else blank
        skips = [skip_sent[tick - wait] if tick >= wait else blank for wait in waits]
        in_flight = skip_sent[tick - soon] if tick >= soon else blank
        output, skip_output, grads, weights = backward_tick(
            base, tick, arrived, head_grads, skips, in_flight, gains, weights, kept, grads
        )
        arriving.append(lax.ppermute(output, BOTH, chain_backward))
        is_needed = tick < LAG * (sections - 2) + slots
        skip_sent.append(lax.ppermute(skip_output, BOTH, skip_backward) if is_needed else blank)

    columns = min(1024, width)
    attn_blocks = [
        ("ain", "qkvg", start, start, columns) for start in range(0, 3 * width, columns)
    ] + [("ctx", "proj", start, 3 * width + start, columns) for start in range(0, width, columns)]
    specs = {
        "down": (
            hidden_size // batch,
            width,
            [("act", "branch", start, start, columns) for start in range(0, width, columns)],
        ),
        "up": (
            width // batch,
            hidden_size,
            [("fin", "hid", start, start, columns) for start in range(0, hidden_size, columns)],
        ),
        "attn": (width // batch, 4 * width, attn_blocks),
        "skip": (
            2 * width // batch,
            width,
            [("join", "resg", start, start, columns) for start in range(0, width, columns)],
        ),
    }
    lefts = dict(zip(("join", "ain", "ctx", "fin", "act"), (kept[i] for i in (0, 2, 5, 7, 8))))
    rights = dict(zip(("branch", "hid", "proj", "qkvg", "resg"), grads))

    def lefts_of(name):
        rows = specs[name][0]
        found = {}
        for left in dict.fromkeys(block[0] for block in specs[name][2]):
            array = lefts[left]
            if rows % 128:
                array = array.reshape(slots, row_len, 4, span, rows)
                array = jnp.moveaxis(array, 3, 0).reshape(span, slots, row_len, 4 * rows)
                array = jnp.pad(array, ((0, 0),) * 3 + ((0, -4 * rows % 128),))
            found[left] = array
        return found

    def products(names, first, came, earlier):
        wanted = dict.fromkeys(block[1] for name in names for block in specs[name][2])
        found = {}
        for name in names:
            found |= lefts_of(name)
        return weight_products(
            base,
            first,
            slots,
            span,
            [specs[name] for name in names],
            found,
            {right: rights[right] for right in wanted},
            came,
            [stay_in_hbm(array) for array in earlier],
        )

    groups = (("skip",), ("up", "down", "attn"))
    came, own_grads, arrived_grads, own_squares = {}, {}, {}, {}
    earlier = []
    for names in groups:
        sent = products(names, True, [], earlier)
        if not earlier:
            table_earlier = sent[0]
        earlier = sent[:1]
        members = (2,) if names == ("skip",) else (1, 2)
        bits = [1 + i % (span - 1) for i in range(len(sent))]
        came[names] = [across(part, bit, members) for part, bit in zip(sent, bits)]

    for names in groups:
        results = products(names, False, came[names], earlier)
        earlier = results[:1]
        limit = (
            (lambda pairs: tuple(p for p in pairs if p[0] >= 2))
            if names == ("skip",)
            else (lambda pairs: pairs)
        )
        arrived_grads[names] = [
            along(part, limit(pairs)) for part, pairs in zip(results, (outward, near, back_far))
        ]
        own_grads |= dict(zip(names, results[3:-1]))
        own_squares[names] = results[-1]

    table_count = front_rows + mel_bins + 1
    table_rows = -(-table_count // (16 * span)) * 16 * span
    shared = table_pass(
        base, flat_front, grads[4], grads[5], head_total, out_gain_total, table_rows, table_earlier
    )
    bit = 1
    while bit < span:
        shared = shared + across(shared, bit)
        bit *= 2
    share = table_rows // span
    mine = lax.dynamic_slice_in_dim(shared, rank * share, share, 0)
    first_rank = (rank == 0) & ~is_outer
    small_squares = jnp.sum(mine.astype(F32) ** 2) + jnp.where(
        first_rank, jnp.sum(shared[table_rows:].astype(F32) ** 2), 0.0
    )
    mine = jnp.concatenate([mine, shared[table_rows:]])
    mine = mine + along(mine, near)
    mine = mine + along(mine, outward)
    gain_rows = mine[share : share + 4].astype(F32)
    mine = mine[:share]
    bit = 1
    while bit < sections:
        mine = mine + flipped(mine, "section", bit)
        bit *= 2
    table_parts = [mine] + [across(mine, bits) for bits in range(1, span)]
    table_grad = jnp.zeros((table_rows, width), BF16)
    for bits, part in enumerate(table_parts):
        table_grad = lax.dynamic_update_slice_in_dim(table_grad, part, (rank ^ bits) * share, 0)
    gain_grad = lax.dynamic_slice_in_dim(
        gain_rows, batch_id * (width // batch), width // batch, 1
    )


    def squares_of(names):
        edge, close, distant = (part.astype(F32) for part in arrived_grads[names])
        inner = jnp.sum(own_squares[names])
        own = jnp.where(is_outer, jnp.sum(edge**2), inner)
        other = jnp.where(is_outer, jnp.sum(distant**2), jnp.sum(close**2))
        return jnp.where(is_dec, own, other) if names == ("skip",) else own + other

    squares = sum(squares_of(names) for names in groups) + small_squares
    loss_local = jnp.where(is_outer, 0.0, jnp.sum(loss_parts))
    lane = lax.broadcasted_iota(jnp.int32, (8, 128), 1)
    sums = jnp.where(lane == 0, squares, jnp.where(lane == 1, loss_local, 0.0))
    for axis, size in (("batch", batch), ("section", sections)):
        bit = 1
        while bit < size:
            sums = sums + flipped(sums, axis, bit)
            bit *= 2
    loss_sum = sums[0, 1]
    grad_norm = jnp.sqrt(sums[0, 0])
    factor = clip_norm / jnp.maximum(grad_norm, clip_norm)

    def both_layers(name):
        index = groups[1].index(name)
        edge, close, distant = (part[index] for part in arrived_grads[groups[1]])
        if name == "down":
            edge, close, distant = (
                jnp.concatenate(
                    [part[:, i * width : (i + 1) * width] for i in range(hidden_size // width)]
                )
                for part in (edge, close, distant)
            )
        own = jnp.where(is_outer, edge.astype(F32), own_grads[name])
        other = jnp.where(is_outer, distant, close).astype(F32)
        return jnp.stack([jnp.where(is_dec, other, own), jnp.where(is_dec, own, other)])[None]

    attn_out = adam_update(attn_w, attn_m, attn_v, both_layers("attn"), factor, rate_matrix)
    up_out = adam_update(up_w, up_m, up_v, both_layers("up"), factor, rate_matrix)
    down_out = adam_update(down_w, down_m, down_v, both_layers("down"), factor, rate_matrix)
    edge, close, distant = (part[0].astype(F32) for part in arrived_grads[groups[0]])
    skip_grad = jnp.where(
        is_dec, jnp.where(is_outer, edge, own_grads["skip"]), jnp.where(is_outer, distant, close)
    )
    skip_out = adam_update(skip_w, skip_m, skip_v, skip_grad[None], factor, rate_matrix)
    table_grad = table_grad[:table_count].astype(F32)
    gain_out = adam_update(gain_w, gain_m, gain_v, gain_grad[None], factor, rate_gain)
    table_out = adam_update(table_w, table_m, table_v, table_grad, factor, rate_table)
    return (
        loss_sum, mask_total, grad_norm,
        *attn_out, *up_out, *down_out, *skip_out, *gain_out, *table_out,
    )


def solution(mesh):
    row_specs = (
        P("batch", None, None),
        P("batch", None, None),
        P("batch", None),
        P("batch", None),
        P("batch", None),
        P("batch"),
    )
    wide = P("section", None, "batch", None)
    flat = P("section", "batch", None)
    gain = P("section", None, "batch")
    return jax.shard_map(
        body,
        mesh=mesh,
        in_specs=row_specs + (wide,) * 9 + (flat,) * 3 + (gain,) * 3 + (P(),) * 3,
        out_specs=(P(),) * 3 + (wide,) * 12 + (flat,) * 4 + (gain,) * 4 + (P(),) * 4,
        check_vma=False,
    )
```

time: 3460 us -> 1100 us (0.32)
  waiting for transfers between devices: 1990 us -> 491 us
  local copies, waits for them, and re-layouts: 440 us -> 23.9 us
  matrix products: 342 us -> 3.47 us
  other arithmetic: 398 us -> 93.1 us
  Pallas kernels: 0 us -> 207 us
  starting transfers between devices: 144 us -> 240 us
  blocking collectives: 69.9 us -> 16.9 us
  loops' own time: 41.1 us -> 0 us
    reduce_scatter x4 -> x0, waiting for transfers between devices: 1010 us -> none  [the longest x1 324 us: body(): lax.psum_scatter(jnp.stack([enc_total[0], dec_total[0]])[None], 'batch',...]
    all_gather x4 -> x0, waiting for transfers between devices: 388 us -> none  [the longest x1 139 us: body(): lax.all_gather(to_low(up_w), 'batch', axis=2, tiled=True)]
    dot_general x88 -> x2, matrix products: 331 us -> 3.47 us  [matmul(): return jnp.dot(left, right, preferred_element_type=F32)]
    pallas_call x0 -> x71, Pallas kernels: none -> 207 us  [the longest x22 95.2 us: backward_tick(): pl.pallas_call(backward_kernel, out_shape=[jax.ShapeDtypeStruct((rows, wi...]
    dynamic_slice x111 -> x1, local copies, waits for them, and re-layouts: 157 us -> 0.01 us  [chain_part(): return lax.dynamic_slice_in_dim(array, rank * slots, slots, 0)]
    psum x1 -> x0, waiting for transfers between devices: 132 us -> none  [body(): lax.psum((table_local, loss_local, layer_squares), ('section', 'batch'))]
    another operation x125 -> x3, local copies, waits for them, and re-layouts: 114 us -> 0.2 us  [the longest x1 0.11 us: body(): times = jnp.stack([time_idx // 32, time_idx % 32], axis=1)]
    dynamic_update_slice x113 -> x1, other arithmetic: 114 us -> 2.08 us  [body(): lax.dynamic_update_slice_in_dim(table_grad, part, (rank ^ bits) * share, 0)]
  transfers between devices with their start and end apart: 26 -> 99, of which waited for: 15 -> 8; matrix products, arithmetic and copies ran while one was open for 16% -> 5% of each run, Pallas kernels for 0% -> 17%
where the time goes in v1:
time: 1100 us; the launch traced here: 1090 us
  waiting for transfers between devices  491 us (45%)
  starting transfers between devices  240 us (22%)
  Pallas kernels  207 us (19%)
  other arithmetic  93.1 us (8%)
  local copies, waits for them, and re-layouts  23.9 us (2%)
  blocking collectives  16.9 us (2%)
  between operations  13.6 us (1%)
    ppermute x14, waiting for transfers between devices, along(): return lax.ppermute(block, 'batch', route)  473 us
    ppermute x14, starting transfers between devices, along(): return lax.ppermute(block, 'batch', route)  161 us
    pallas_call x22, Pallas kernels, backward_tick(): pl.pallas_call(backward_kernel, out_shape=[jax.ShapeDtypeStruct((rows, wi...  95.2 us
    pallas_call x22, Pallas kernels, forward_tick(): pl.pallas_call(forward_kernel, out_shape=[jax.ShapeDtypeStruct((rows, wid...  89.6 us
    convert_element_type x6, other arithmetic, adam_update(): return (master_new, first_new, second_new, master_new.astype(BF16))  38.5 us
    ppermute x14, starting transfers between devices, across(): return lax.ppermute(block, 'batch', route)  22.3 us
  transfers between devices with their start and end apart: 99, of which 8 were waited for; matrix products, arithmetic and copies ran while one was open for 5% of the time, Pallas kernels for 17%

profile of v1, /device:TPU:0, one launch (start us, length us, event | category | flops | bytes accessed | tf_op | source)
XLA Modules:
  0.0 1088.6 jit_solution(8847229881787464351)
XLA Ops:
  8.7 16.9 %all_gather.3 = bf16[8,336,128]{2,1,0:T(8,128)(2,1)S(1)} all-gather(bf16[1,336,128]{2,1,0:T(8,128)(2,1)S(1)} %pad_bitcast_fusion), channel_id=1, replica_groups=mesh['section'=4,'batch'=8] {'batch'}, dimensions={0}, use_global_device_ids=true | all-gather | bytes 774144 | tf_op jit(solution)/shard_map/all_gather | solution.py:1085
  51.7 135.3 %collective-permute-start.9 = (bf16[256,1024]{1,0:T(8,128)(2,1)S(1)}, bf16[256,1024]{1,0:T(8,128)(2,1)}, u32[]{:S(2)}, u32[]{:S(2)}) collective-permute-start(bf16[256,1024]{1,0:T(8,128)(2,1)S(1)} %copy-done.17), channel_id=1, source_target_pairs={{0,4},{1,5},{8,12},{9,13},{16,20},{17,21},{24,28},{25,29}} | collective-permute-start | bytes 1572872 | tf_op jit(solution)/shard_map/ppermute | solution.py:1051
  219.1 7.2 layer_forward.22
  230.3 7.9 layer_forward.24
  243.4 7.6 layer_forward.26
  255.7 7.1 layer_forward.28
  276.0 6.6 layer_forward.32
  286.1 6.9 layer_forward.34
  296.3 7.5 layer_forward.36
  307.2 7.7 layer_forward.38
  318.2 6.9 layer_forward.40
  327.7 10.2 layer_forward.42
  344.7 9.0 layer_backward.23
  357.2 6.7 layer_backward.25
  367.5 6.8 layer_backward.27
  377.8 7.0 layer_backward.29
  388.3 6.7 layer_backward.31
  398.5 7.0 layer_backward.33
  409.1 6.6 layer_backward.35
  417.8 8.0 layer_backward.37
  427.9 8.2 layer_backward.39
  438.3 7.9 layer_backward.41
  447.6 13.4 %layer_backward.43 = (bf16[128,1024]{1,0:T(8,128)(2,1)}, bf16[128,1024]{1,0:T(8,128)(2,1)}, bf16[8,128,1024]{2,1,0:T(8,128)(2,1)}, bf16[8,128,4096]{2,1,0:T(8,12...) custom-call(s32[10]{0:T(128)S(1)} %stack.110.base_ref.base, ...), custom_call_target="tpu_custom_call", output_to_operand_aliasing={{2}: (18, {}), {3}: (19, {}), {4}: (20, {}), {5}: (21, {}),... | custom-call | flops 1 | bytes 1 | tf_op jit(solution)/shard_map/layer_backward/pallas_call | solution.py:496
  480.4 7.7 weight_products.7
  494.7 357.2 %collective-permute-done.95 = bf16[272,1024]{1,0:T(8,128)(2,1)S(1)} collective-permute-done((bf16[272,1024]{1,0:T(8,128)(2,1)S(1)}, bf16[272,1024]{1,0:T(8,128)(2,1)S(1)}, u32[]{:S(2)}, u32[]{:S(2)}) %collective-permute-start.95) | collective-permute-done | bytes 557088 | tf_op jit(solution)/shard_map/ppermute | solution.py:1051
  856.2 8.7 collective-permute-done.96
  865.0 115.5 %collective-permute-done.80 = bf16[1,256,1024]{2,1,0:T(8,128)(2,1)S(1)} collective-permute-done((bf16[1,256,1024]{2,1,0:T(8,128)(2,1)S(1)}, bf16[1,256,1024]{2,1,0:T(8,128)(2,1)S(1)}, u32[]{:S(2)}, u32[]{:S(2)}) %collective-permute-start.80) | collective-permute-done | bytes 524320 | tf_op jit(solution)/shard_map/ppermute | solution.py:1051
  1017.1 7.0 fusion.7
  1046.0 7.5 fusion.38
  1054.4 8.6 fusion.44
  1063.1 11.2 %fusion.46 = (bf16[1,2,128,4096]{3,2,1,0:T(8,128)(2,1)}, f32[1,2,128,4096]{3,2,1,0:T(8,128)}, f32[1,2,128,4096]{3,2,1,0:T(8,128)}, f32[1,2,128,4096]{3,2,1,0:T(8,128)}) fusion(f32[1,2,128,4096]{3,2,1,0:T(8,128)S(1)} %copy-done.6, f32[]{:T(128)S(6)} %div.127, f32[1,1,128,4096]{3,2,1,0:T(8,128)S(1)} %copy-done.15, f32[1,1,128,4096]{3,2,1,0:T(8,128)S(1)} %copy-done.14, ...), kind=kLoop, calls=%fused_computation.165 | loop fusion | flops 18874368 | bytes 31457284 | tf_op jit(solution)/shard_map/convert_element_type | solution.py:997
  1076.4 6.9 fusion.48
  (462 shorter events, 229.6 us)
Async XLA Ops:
  31.5 157.8 %collective-permute-start.1 = (bf16[3,128,4096]{2,1,0:T(8,128)(2,1)}, bf16[3,128,4096]{2,1,0:T(8,128)(2,1)}, u32[]{:S(2)}, u32[]{:S(2)}) collective-permute-start(bf16[3,128,4096]{2,1,0:T(8,128)(2,1)} %ordered.4), channel_id=1, source_target_pairs={{2,4},{3,5},{4,2},{5,3},{10,12},{11,13},{12,10},{13,11},{18,20},{1... | collective-permute-start | bytes 9437192 | tf_op jit(solution)/shard_map/ppermute | solution.py:1051
  34.8 156.8 %collective-permute-start.2 = (bf16[3,128,4096]{2,1,0:T(8,128)(2,1)}, bf16[3,128,4096]{2,1,0:T(8,128)(2,1)}, u32[]{:S(2)}, u32[]{:S(2)}) collective-permute-start(bf16[3,128,4096]{2,1,0:T(8,128)(2,1)} %ordered.4), channel_id=1, source_target_pairs={{0,4},{1,5},{6,2},{7,3},{8,12},{9,13},{14,10},{15,11},{16,20},{17,... | collective-permute-start | bytes 9437192 | tf_op jit(solution)/shard_map/ppermute | solution.py:1051
  44.0 142.9 %collective-permute-start = (bf16[3,128,4096]{2,1,0:T(8,128)(2,1)}, bf16[3,128,4096]{2,1,0:T(8,128)(2,1)}, u32[]{:S(2)}, u32[]{:S(2)}) collective-permute-start(bf16[3,128,4096]{2,1,0:T(8,128)(2,1)} %ordered.3.refs_0_), channel_id=1, source_target_pairs={{0,2},{1,3},{6,4},{7,5},{8,10},{9,11},{14,12},{15,13},{16,18},{17,... | collective-permute-start | bytes 9437192 | tf_op jit(solution)/shard_map/ppermute | solution.py:1051
  49.3 167.4 %collective-permute-start.3 = (bf16[3,128,4096]{2,1,0:T(8,128)(2,1)}, bf16[3,128,4096]{2,1,0:T(8,128)(2,1)}, u32[]{:S(2)}, u32[]{:S(2)}) collective-permute-start(bf16[3,128,4096]{2,1,0:T(8,128)(2,1)} %ordered.3.refs_0_), channel_id=1, source_target_pairs={{2,3},{3,2},{4,5},{5,4},{10,11},{11,10},{12,13},{13,12},{18,19},{1... | collective-permute-start | bytes 9437192 | tf_op jit(solution)/shard_map/ppermute | solution.py:1055
  51.7 150.9 %collective-permute-start.9 = (bf16[256,1024]{1,0:T(8,128)(2,1)S(1)}, bf16[256,1024]{1,0:T(8,128)(2,1)}, u32[]{:S(2)}, u32[]{:S(2)}) collective-permute-start(bf16[256,1024]{1,0:T(8,128)(2,1)S(1)} %copy-done.17), channel_id=1, source_target_pairs={{0,4},{1,5},{8,12},{9,13},{16,20},{17,21},{24,28},{25,29}} | collective-permute-start | bytes 1572872 | tf_op jit(solution)/shard_map/ppermute | solution.py:1051
  187.0 29.7 %collective-permute-start.4 = (bf16[3,128,4096]{2,1,0:T(8,128)(2,1)}, bf16[3,128,4096]{2,1,0:T(8,128)(2,1)}, u32[]{:S(2)}, u32[]{:S(2)}) collective-permute-start(bf16[3,128,4096]{2,1,0:T(8,128)(2,1)} %collective-permute-done.refs_1_), channel_id=1, source_target_pairs={{2,3},{3,2},{4,5},{5,4},{10,11},{11,10},{12,13},{13,12},{18,19},{1... | collective-permute-start | bytes 9437192 | tf_op jit(solution)/shard_map/ppermute | solution.py:1055
  189.3 27.3 %collective-permute-start.5 = (bf16[3,128,4096]{2,1,0:T(8,128)(2,1)}, bf16[3,128,4096]{2,1,0:T(8,128)(2,1)}, u32[]{:S(2)}, u32[]{:S(2)}) collective-permute-start(bf16[3,128,4096]{2,1,0:T(8,128)(2,1)} %collective-permute-done.1.refs_2_), channel_id=1, source_target_pairs={{2,3},{3,2},{4,5},{5,4},{10,11},{11,10},{12,13},{13,12},{18,19},{1... | collective-permute-start | bytes 9437192 | tf_op jit(solution)/shard_map/ppermute | solution.py:1055
  191.6 25.0 %collective-permute-start.6 = (bf16[3,128,4096]{2,1,0:T(8,128)(2,1)}, bf16[3,128,4096]{2,1,0:T(8,128)(2,1)}, u32[]{:S(2)}, u32[]{:S(2)}) collective-permute-start(bf16[3,128,4096]{2,1,0:T(8,128)(2,1)} %collective-permute-done.2.refs_3_), channel_id=1, source_target_pairs={{2,3},{3,2},{4,5},{5,4},{10,11},{11,10},{12,13},{13,12},{18,19},{1... | collective-permute-start | bytes 9437192 | tf_op jit(solution)/shard_map/ppermute | solution.py:1055
  228.3 11.8 %collective-permute-start.14 = (bf16[128,1024]{1,0:T(8,128)(2,1)S(1)}, bf16[128,1024]{1,0:T(8,128)(2,1)S(1)}, u32[]{:S(2)}, u32[]{:S(2)}) collective-permute-start(bf16[128,1024]{1,0:T(8,128)(2,1)S(1)} %get-tuple-element.743), channel_id=1, source_target_pairs={{2,10},{3,11},{10,18},{11,19},{18,26},{19,27},{26,28},{27,29},{28,... | collective-permute-start | bytes 786440 | tf_op jit(solution)/shard_map/ppermute | solution.py:1192
  229.0 13.8 %collective-permute-start.19 = (bf16[128,1024]{1,0:T(8,128)(2,1)S(1)}, bf16[128,1024]{1,0:T(8,128)(2,1)S(1)}, u32[]{:S(2)}, u32[]{:S(2)}) collective-permute-start(bf16[128,1024]{1,0:T(8,128)(2,1)S(1)} %get-tuple-element.744), channel_id=1, source_target_pairs={{2,4},{3,5},{10,12},{11,13},{18,20},{19,21}} | collective-permute-start | bytes 786440 | tf_op jit(solution)/shard_map/ppermute | solution.py:1194
  238.8 13.5 %collective-permute-start.17 = (bf16[128,1024]{1,0:T(8,128)(2,1)S(1)}, bf16[128,1024]{1,0:T(8,128)(2,1)S(1)}, u32[]{:S(2)}, u32[]{:S(2)}) collective-permute-start(bf16[128,1024]{1,0:T(8,128)(2,1)S(1)} %get-tuple-element.743), channel_id=1, source_target_pairs={{2,4},{3,5},{10,12},{11,13},{18,20},{19,21}} | collective-permute-start | bytes 786440 | tf_op jit(solution)/shard_map/ppermute | solution.py:1194
  240.8 11.6 %collective-permute-start.16 = (bf16[128,1024]{1,0:T(8,128)(2,1)S(1)}, bf16[128,1024]{1,0:T(8,128)(2,1)S(1)}, u32[]{:S(2)}, u32[]{:S(2)}) collective-permute-start(bf16[128,1024]{1,0:T(8,128)(2,1)S(1)} %get-tuple-element.779), channel_id=1, source_target_pairs={{2,10},{3,11},{10,18},{11,19},{18,26},{19,27},{26,28},{27,29},{28,... | collective-permute-start | bytes 786440 | tf_op jit(solution)/shard_map/ppermute | solution.py:1192
  241.5 13.5 %collective-permute-start.23 = (bf16[128,1024]{1,0:T(8,128)(2,1)S(1)}, bf16[128,1024]{1,0:T(8,128)(2,1)S(1)}, u32[]{:S(2)}, u32[]{:S(2)}) collective-permute-start(bf16[128,1024]{1,0:T(8,128)(2,1)S(1)} %get-tuple-element.780), channel_id=1, source_target_pairs={{2,4},{3,5},{10,12},{11,13},{18,20},{19,21}} | collective-permute-start | bytes 786440 | tf_op jit(solution)/shard_map/ppermute | solution.py:1194
  242.8 21.3 %collective-permute-start.21 = (bf16[128,1024]{1,0:T(8,128)(2,1)S(1)}, bf16[128,1024]{1,0:T(8,128)(2,1)S(1)}, u32[]{:S(2)}, u32[]{:S(2)}) collective-permute-start(bf16[128,1024]{1,0:T(8,128)(2,1)S(1)} %get-tuple-element.779), channel_id=1, source_target_pairs={{2,4},{3,5},{10,12},{11,13},{18,20},{19,21}} | collective-permute-start | bytes 786440 | tf_op jit(solution)/shard_map/ppermute | solution.py:1194
  253.8 12.4 %collective-permute-start.27 = (bf16[128,1024]{1,0:T(8,128)(2,1)S(1)}, bf16[128,1024]{1,0:T(8,128)(2,1)S(1)}, u32[]{:S(2)}, u32[]{:S(2)}) collective-permute-start(bf16[128,1024]{1,0:T(8,128)(2,1)S(1)} %get-tuple-element.816), channel_id=1, source_target_pairs={{2,4},{3,5},{10,12},{11,13},{18,20},{19,21}} | collective-permute-start | bytes 786440 | tf_op jit(solution)/shard_map/ppermute | solution.py:1194
  255.0 18.8 %collective-permute-start.25 = (bf16[128,1024]{1,0:T(8,128)(2,1)S(1)}, bf16[128,1024]{1,0:T(8,128)(2,1)S(1)}, u32[]{:S(2)}, u32[]{:S(2)}) collective-permute-start(bf16[128,1024]{1,0:T(8,128)(2,1)S(1)} %get-tuple-element.815), channel_id=1, source_target_pairs={{2,4},{3,5},{10,12},{11,13},{18,20},{19,21}} | collective-permute-start | bytes 786440 | tf_op jit(solution)/shard_map/ppermute | solution.py:1194
  365.4 12.4 %collective-permute-start.53 = (bf16[128,1024]{1,0:T(8,128)(2,1)S(1)}, bf16[128,1024]{1,0:T(8,128)(2,1)S(1)}, u32[]{:S(2)}, u32[]{:S(2)}) collective-permute-start(bf16[128,1024]{1,0:T(8,128)(2,1)S(1)} %get-tuple-element.1171), channel_id=1, source_target_pairs={{4,2},{5,3},{12,10},{13,11},{20,18},{21,19}} | collective-permute-start | bytes 786440 | tf_op jit(solution)/shard_map/ppermute | solution.py:1213
  375.7 12.6 %collective-permute-start.57 = (bf16[128,1024]{1,0:T(8,128)(2,1)S(1)}, bf16[128,1024]{1,0:T(8,128)(2,1)S(1)}, u32[]{:S(2)}, u32[]{:S(2)}) collective-permute-start(bf16[128,1024]{1,0:T(8,128)(2,1)S(1)} %get-tuple-element.1195), channel_id=1, source_target_pairs={{4,2},{5,3},{12,10},{13,11},{20,18},{21,19}} | collective-permute-start | bytes 786440 | tf_op jit(solution)/shard_map/ppermute | solution.py:1213
  386.2 12.4 %collective-permute-start.61 = (bf16[128,1024]{1,0:T(8,128)(2,1)S(1)}, bf16[128,1024]{1,0:T(8,128)(2,1)S(1)}, u32[]{:S(2)}, u32[]{:S(2)}) collective-permute-start(bf16[128,1024]{1,0:T(8,128)(2,1)S(1)} %get-tuple-element.1219), channel_id=1, source_target_pairs={{4,2},{5,3},{12,10},{13,11},{20,18},{21,19}} | collective-permute-start | bytes 786440 | tf_op jit(solution)/shard_map/ppermute | solution.py:1213
  396.4 12.6 %collective-permute-start.65 = (bf16[128,1024]{1,0:T(8,128)(2,1)S(1)}, bf16[128,1024]{1,0:T(8,128)(2,1)S(1)}, u32[]{:S(2)}, u32[]{:S(2)}) collective-permute-start(bf16[128,1024]{1,0:T(8,128)(2,1)S(1)} %get-tuple-element.1243), channel_id=1, source_target_pairs={{4,2},{5,3},{12,10},{13,11},{20,18},{21,19}} | collective-permute-start | bytes 786440 | tf_op jit(solution)/shard_map/ppermute | solution.py:1213
  462.7 17.6 %collective-permute-start.82 = (bf16[4,128,4096]{2,1,0:T(8,128)(2,1)}, bf16[4,128,4096]{2,1,0:T(8,128)(2,1)}, u32[]{:S(2)}, u32[]{:S(2)}) collective-permute-start(bf16[4,128,4096]{2,1,0:T(8,128)(2,1)} %get-tuple-element.1365.refs_3_), channel_id=1, source_target_pairs={{2,3},{3,2},{4,5},{5,4},{10,11},{11,10},{12,13},{13,12},{18,19},{1... | collective-permute-start | bytes 12582920 | tf_op jit(solution)/shard_map/ppermute | solution.py:1055
  465.4 15.0 %collective-permute-start.83 = (bf16[4,512,1024]{2,1,0:T(8,128)(2,1)}, bf16[4,512,1024]{2,1,0:T(8,128)(2,1)}, u32[]{:S(2)}, u32[]{:S(2)}) collective-permute-start(bf16[4,512,1024]{2,1,0:T(8,128)(2,1)} %get-tuple-element.1370), channel_id=1, source_target_pairs={{2,3},{3,2},{4,5},{5,4},{10,11},{11,10},{12,13},{13,12},{18,19},{1... | collective-permute-start | bytes 12582920 | tf_op jit(solution)/shard_map/ppermute | solution.py:1055
  468.0 12.3 %collective-permute-start.84 = (bf16[4,128,4096]{2,1,0:T(8,128)(2,1)}, bf16[4,128,4096]{2,1,0:T(8,128)(2,1)}, u32[]{:S(2)}, u32[]{:S(2)}) collective-permute-start(bf16[4,128,4096]{2,1,0:T(8,128)(2,1)} %get-tuple-element.1371), channel_id=1, source_target_pairs={{2,3},{3,2},{4,5},{5,4},{10,11},{11,10},{12,13},{13,12},{18,19},{1... | collective-permute-start | bytes 12582920 | tf_op jit(solution)/shard_map/ppermute | solution.py:1055
  478.9 13.0 %collective-permute-start.94 = (bf16[272,1024]{1,0:T(8,128)(2,1)S(1)}, bf16[272,1024]{1,0:T(8,128)(2,1)S(1)}, u32[]{:S(2)}, u32[]{:S(2)}) collective-permute-start(bf16[272,1024]{1,0:T(8,128)(2,1)S(1)} %pad_maximum_fusion.4), channel_id=1, source_target_pairs={{2,4},{3,5},{4,2},{5,3},{10,12},{11,13},{12,10},{13,11},{18,20},{1... | collective-permute-start | bytes 1671176 | tf_op jit(solution)/shard_map/ppermute | solution.py:1051
  488.1 509.3 %collective-permute-start.87 = (bf16[3,128,4096]{2,1,0:T(8,128)(2,1)}, bf16[3,128,4096]{2,1,0:T(8,128)(2,1)}, u32[]{:S(2)}, u32[]{:S(2)}) collective-permute-start(bf16[3,128,4096]{2,1,0:T(8,128)(2,1)} %get-tuple-element.1375), channel_id=1, source_target_pairs={{2,4},{3,5},{4,2},{5,3},{10,12},{11,13},{12,10},{13,11},{18,20},{1... | collective-permute-start | bytes 9437192 | tf_op jit(solution)/shard_map/ppermute | solution.py:1051
  490.6 511.0 %collective-permute-start.86 = (bf16[3,128,4096]{2,1,0:T(8,128)(2,1)}, bf16[3,128,4096]{2,1,0:T(8,128)(2,1)}, u32[]{:S(2)}, u32[]{:S(2)}) collective-permute-start(bf16[3,128,4096]{2,1,0:T(8,128)(2,1)} %get-tuple-element.1374), channel_id=1, source_target_pairs={{2,6},{3,7},{4,0},{5,1},{10,14},{11,15},{12,8},{13,9},{18,22},{19,... | collective-permute-start | bytes 9437192 | tf_op jit(solution)/shard_map/ppermute | solution.py:1051
  492.1 359.8 %collective-permute-start.95 = (bf16[272,1024]{1,0:T(8,128)(2,1)S(1)}, bf16[272,1024]{1,0:T(8,128)(2,1)S(1)}, u32[]{:S(2)}, u32[]{:S(2)}) collective-permute-start(bf16[272,1024]{1,0:T(8,128)(2,1)S(1)} %fusion.37), channel_id=1, source_target_pairs={{2,0},{3,1},{4,6},{5,7},{10,8},{11,9},{12,14},{13,15},{18,16},{19,... | collective-permute-start | bytes 1671176 | tf_op jit(solution)/shard_map/ppermute | solution.py:1051
  493.4 513.6 %collective-permute-start.85 = (bf16[3,128,4096]{2,1,0:T(8,128)(2,1)}, bf16[3,128,4096]{2,1,0:T(8,128)(2,1)}, u32[]{:S(2)}, u32[]{:S(2)}) collective-permute-start(bf16[3,128,4096]{2,1,0:T(8,128)(2,1)} %get-tuple-element.1372), channel_id=1, source_target_pairs={{2,0},{3,1},{4,6},{5,7},{10,8},{11,9},{12,14},{13,15},{18,16},{19,... | collective-permute-start | bytes 9437192 | tf_op jit(solution)/shard_map/ppermute | solution.py:1051
  852.2 12.6 %collective-permute-start.96 = (bf16[256,1024]{1,0:T(8,128)(2,1)S(1)}, bf16[256,1024]{1,0:T(8,128)(2,1)S(1)}, u32[]{:S(2)}, u32[]{:S(2)}) collective-permute-start(bf16[256,1024]{1,0:T(8,128)(2,1)S(1)} %slice.332), channel_id=1, source_target_pairs={{0,8},{8,0},{16,24},{24,16},{1,9},{9,1},{17,25},{25,17},{2,10},{10... | collective-permute-start | bytes 1572872 | tf_op jit(solution)/shard_map/ppermute | solution.py:1058
  854.9 125.6 %collective-permute-start.80 = (bf16[1,256,1024]{2,1,0:T(8,128)(2,1)S(1)}, bf16[1,256,1024]{2,1,0:T(8,128)(2,1)S(1)}, u32[]{:S(2)}, u32[]{:S(2)}) collective-permute-start(bf16[1,256,1024]{2,1,0:T(8,128)(2,1)S(1)} %copy-done.56), channel_id=1, source_target_pairs={{4,0},{5,1},{12,8},{13,9},{20,16},{21,17},{28,24},{29,25}} | collective-permute-start | bytes 1572872 | tf_op jit(solution)/shard_map/ppermute | solution.py:1051
  864.9 117.6 %collective-permute-start.97 = (bf16[256,1024]{1,0:T(8,128)(2,1)S(1)}, bf16[256,1024]{1,0:T(8,128)(2,1)S(1)}, u32[]{:S(2)}, u32[]{:S(2)}) collective-permute-start(bf16[256,1024]{1,0:T(8,128)(2,1)S(1)} %slice_add_fusion.1), channel_id=1, source_target_pairs={{0,16},{8,24},{16,0},{24,8},{1,17},{9,25},{17,1},{25,9},{2,18},{10... | collective-permute-start | bytes 1572872 | tf_op jit(solution)/shard_map/ppermute | solution.py:1058
  1012.6 11.6 %collective-permute-start.89 = (f32[8,128]{1,0:T(8,128)S(1)}, f32[8,128]{1,0:T(8,128)S(1)}, u32[]{:S(2)}, u32[]{:S(2)}) collective-permute-start(f32[8,128]{1,0:T(8,128)S(1)} %broadcast_select_fusion.2), channel_id=1, source_target_pairs={{0,1},{1,0},{2,3},{3,2},{4,5},{5,4},{6,7},{7,6},{8,9},{9,8},{10,11... | collective-permute-start | bytes 12296 | tf_op jit(solution)/shard_map/ppermute | solution.py:1058
  (128 other events, 2317.5 us)

commit v2 on v1

--- a/solution.py
+++ b/solution.py
@@ -1327,10 +1327,9 @@
 
     def squares_of(names):
         edge, close, distant = (part.astype(F32) for part in arrived_grads[names])
-        inner = jnp.sum(own_squares[names])
-        own = jnp.where(is_outer, jnp.sum(edge**2), inner)
-        other = jnp.where(is_outer, jnp.sum(distant**2), jnp.sum(close**2))
-        return jnp.where(is_dec, own, other) if names == ("skip",) else own + other
+        has_own = (quarter == 2) if names == ("skip",) else ~is_outer
+        own = jnp.where(has_own, jnp.sum(own_squares[names]), 0.0)
+        return own + jnp.sum(edge * edge + close * close + distant * distant)
 
     squares = sum(squares_of(names) for names in groups) + small_squares
     loss_local = jnp.where(is_outer, 0.0, jnp.sum(loss_parts))

time: 1100 us -> 1120 us (1.018)
  waiting for transfers between devices: 491 us -> 527 us
    ppermute x14, waiting for transfers between devices: 473 us -> 492 us  [along(): return lax.ppermute(block, 'batch', route)]
    ppermute x7, waiting for transfers between devices: 15.5 us -> 32.8 us  [flipped(): lax.ppermute(block, axis, [(i, i ^ bit) for i in range(lax.axis_size(axis...]
  transfers between devices with their start and end apart: 99 -> 99, of which waited for: 8 -> 9; matrix products, arithmetic and copies ran while one was open for 5% -> 4% of each run, Pallas kernels for 17% -> 16%
where the time goes in v2:
time: 1120 us; the launch traced here: 1100 us
  waiting for transfers between devices  527 us (47%)
  starting transfers between devices  231 us (21%)
  Pallas kernels  206 us (18%)
  other arithmetic  85.4 us (8%)
  local copies, waits for them, and re-layouts  24 us (2%)
  blocking collectives  16.9 us (2%)
    ppermute x14, waiting for transfers between devices, along(): return lax.ppermute(block, 'batch', route)  492 us
    ppermute x14, starting transfers between devices, along(): return lax.ppermute(block, 'batch', route)  161 us
    pallas_call x22, Pallas kernels, backward_tick(): pl.pallas_call(backward_kernel, out_shape=[jax.ShapeDtypeStruct((rows, wi...  95.2 us
    pallas_call x22, Pallas kernels, forward_tick(): pl.pallas_call(forward_kernel, out_shape=[jax.ShapeDtypeStruct((rows, wid...  89.6 us
    convert_element_type x6, other arithmetic, adam_update(): return (master_new, first_new, second_new, master_new.astype(BF16))  38.7 us
    ppermute x7, waiting for transfers between devices, flipped(): lax.ppermute(block, axis, [(i, i ^ bit) for i in range(lax.axis_size(axis...  32.8 us
  transfers between devices with their start and end apart: 99, of which 9 were waited for; matrix products, arithmetic and copies ran while one was open for 4% of the time, Pallas kernels for 16%

profile of v2, /device:TPU:0, one launch (start us, length us, event | category | flops | bytes accessed | tf_op | source)
XLA Modules:
  0.0 1104.6 jit_solution(3798776151839503348)
XLA Ops:
  8.7 16.9 %all_gather.3 = bf16[8,336,128]{2,1,0:T(8,128)(2,1)S(1)} all-gather(bf16[1,336,128]{2,1,0:T(8,128)(2,1)S(1)} %pad_bitcast_fusion), channel_id=1, replica_groups=mesh['section'=4,'batch'=8] {'batch'}, dimensions={0}, use_global_device_ids=true | all-gather | bytes 774144 | tf_op jit(solution)/shard_map/all_gather | solution.py:1085
  51.6 135.3 %collective-permute-start.9 = (bf16[256,1024]{1,0:T(8,128)(2,1)S(1)}, bf16[256,1024]{1,0:T(8,128)(2,1)}, u32[]{:S(2)}, u32[]{:S(2)}) collective-permute-start(bf16[256,1024]{1,0:T(8,128)(2,1)S(1)} %copy-done.17), channel_id=1, source_target_pairs={{0,4},{1,5},{8,12},{9,13},{16,20},{17,21},{24,28},{25,29}} | collective-permute-start | bytes 1572872 | tf_op jit(solution)/shard_map/ppermute | solution.py:1051
  219.0 7.2 layer_forward.22
  230.2 7.9 layer_forward.24
  243.4 7.6 layer_forward.26
  255.7 7.1 layer_forward.28
  276.0 6.6 layer_forward.32
  286.0 6.9 layer_forward.34
  296.3 7.5 layer_forward.36
  307.1 7.7 layer_forward.38
  318.1 6.9 layer_forward.40
  327.7 10.2 layer_forward.42
  344.7 9.0 layer_backward.23
  357.2 6.7 layer_backward.25
  367.4 6.8 layer_backward.27
  377.7 7.0 layer_backward.29
  388.2 6.7 layer_backward.31
  398.5 7.0 layer_backward.33
  409.0 6.6 layer_backward.35
  417.8 8.0 layer_backward.37
  427.9 8.2 layer_backward.39
  438.2 7.9 layer_backward.41
  447.6 13.4 %layer_backward.43 = (bf16[128,1024]{1,0:T(8,128)(2,1)}, bf16[128,1024]{1,0:T(8,128)(2,1)}, bf16[8,128,1024]{2,1,0:T(8,128)(2,1)}, bf16[8,128,4096]{2,1,0:T(8,12...) custom-call(s32[10]{0:T(128)S(1)} %stack.110.base_ref.base, ...), custom_call_target="tpu_custom_call", output_to_operand_aliasing={{2}: (18, {}), {3}: (19, {}), {4}: (20, {}), {5}: (21, {}),... | custom-call | flops 1 | bytes 1 | tf_op jit(solution)/shard_map/layer_backward/pallas_call | solution.py:496
  480.3 6.7 weight_products.7
  493.6 485.4 %collective-permute-done.95 = bf16[272,1024]{1,0:T(8,128)(2,1)S(1)} collective-permute-done((bf16[272,1024]{1,0:T(8,128)(2,1)S(1)}, bf16[272,1024]{1,0:T(8,128)(2,1)S(1)}, u32[]{:S(2)}, u32[]{:S(2)}) %collective-permute-start.95) | collective-permute-done | bytes 557088 | tf_op jit(solution)/shard_map/ppermute | solution.py:1051
  982.8 11.0 collective-permute-done.96
  995.5 11.3 %collective-permute-done.97 = bf16[256,1024]{1,0:T(8,128)(2,1)S(1)} collective-permute-done((bf16[256,1024]{1,0:T(8,128)(2,1)S(1)}, bf16[256,1024]{1,0:T(8,128)(2,1)S(1)}, u32[]{:S(2)}, u32[]{:S(2)}) %collective-permute-start.97) | collective-permute-done | bytes 524320 | tf_op jit(solution)/shard_map/ppermute | solution.py:1058
  1037.9 7.0 fusion.7
  1061.9 7.5 fusion.38
  1070.3 8.6 fusion.44
  1078.9 11.2 %fusion.46 = (bf16[1,2,128,4096]{3,2,1,0:T(8,128)(2,1)}, f32[1,2,128,4096]{3,2,1,0:T(8,128)}, f32[1,2,128,4096]{3,2,1,0:T(8,128)}, f32[1,2,128,4096]{3,2,1,0:T(8,128)}) fusion(f32[1,2,128,4096]{3,2,1,0:T(8,128)S(1)} %copy-done.6, f32[]{:T(128)S(6)} %div.127, f32[1,1,128,4096]{3,2,1,0:T(8,128)S(1)} %copy-done.15, f32[1,1,128,4096]{3,2,1,0:T(8,128)S(1)} %copy-done.14, ...), kind=kLoop, calls=%fused_computation.163 | loop fusion | flops 18874368 | bytes 31457284 | tf_op jit(solution)/shard_map/convert_element_type | solution.py:997
  1092.2 6.9 fusion.48
  (454 shorter events, 222.9 us)
Async XLA Ops:
  31.5 157.7 %collective-permute-start.1 = (bf16[3,128,4096]{2,1,0:T(8,128)(2,1)}, bf16[3,128,4096]{2,1,0:T(8,128)(2,1)}, u32[]{:S(2)}, u32[]{:S(2)}) collective-permute-start(bf16[3,128,4096]{2,1,0:T(8,128)(2,1)} %ordered.4), channel_id=1, source_target_pairs={{2,4},{3,5},{4,2},{5,3},{10,12},{11,13},{12,10},{13,11},{18,20},{1... | collective-permute-start | bytes 9437192 | tf_op jit(solution)/shard_map/ppermute | solution.py:1051
  34.8 156.8 %collective-permute-start.2 = (bf16[3,128,4096]{2,1,0:T(8,128)(2,1)}, bf16[3,128,4096]{2,1,0:T(8,128)(2,1)}, u32[]{:S(2)}, u32[]{:S(2)}) collective-permute-start(bf16[3,128,4096]{2,1,0:T(8,128)(2,1)} %ordered.4), channel_id=1, source_target_pairs={{0,4},{1,5},{6,2},{7,3},{8,12},{9,13},{14,10},{15,11},{16,20},{17,... | collective-permute-start | bytes 9437192 | tf_op jit(solution)/shard_map/ppermute | solution.py:1051
  44.1 142.9 %collective-permute-start = (bf16[3,128,4096]{2,1,0:T(8,128)(2,1)}, bf16[3,128,4096]{2,1,0:T(8,128)(2,1)}, u32[]{:S(2)}, u32[]{:S(2)}) collective-permute-start(bf16[3,128,4096]{2,1,0:T(8,128)(2,1)} %ordered.3.refs_0_), channel_id=1, source_target_pairs={{0,2},{1,3},{6,4},{7,5},{8,10},{9,11},{14,12},{15,13},{16,18},{17,... | collective-permute-start | bytes 9437192 | tf_op jit(solution)/shard_map/ppermute | solution.py:1051
  49.3 167.3 %collective-permute-start.3 = (bf16[3,128,4096]{2,1,0:T(8,128)(2,1)}, bf16[3,128,4096]{2,1,0:T(8,128)(2,1)}, u32[]{:S(2)}, u32[]{:S(2)}) collective-permute-start(bf16[3,128,4096]{2,1,0:T(8,128)(2,1)} %ordered.3.refs_0_), channel_id=1, source_target_pairs={{2,3},{3,2},{4,5},{5,4},{10,11},{11,10},{12,13},{13,12},{18,19},{1... | collective-permute-start | bytes 9437192 | tf_op jit(solution)/shard_map/ppermute | solution.py:1055
  51.6 150.9 %collective-permute-start.9 = (bf16[256,1024]{1,0:T(8,128)(2,1)S(1)}, bf16[256,1024]{1,0:T(8,128)(2,1)}, u32[]{:S(2)}, u32[]{:S(2)}) collective-permute-start(bf16[256,1024]{1,0:T(8,128)(2,1)S(1)} %copy-done.17), channel_id=1, source_target_pairs={{0,4},{1,5},{8,12},{9,13},{16,20},{17,21},{24,28},{25,29}} | collective-permute-start | bytes 1572872 | tf_op jit(solution)/shard_map/ppermute | solution.py:1051
  186.9 29.7 %collective-permute-start.4 = (bf16[3,128,4096]{2,1,0:T(8,128)(2,1)}, bf16[3,128,4096]{2,1,0:T(8,128)(2,1)}, u32[]{:S(2)}, u32[]{:S(2)}) collective-permute-start(bf16[3,128,4096]{2,1,0:T(8,128)(2,1)} %collective-permute-done.refs_1_), channel_id=1, source_target_pairs={{2,3},{3,2},{4,5},{5,4},{10,11},{11,10},{12,13},{13,12},{18,19},{1... | collective-permute-start | bytes 9437192 | tf_op jit(solution)/shard_map/ppermute | solution.py:1055
  189.3 27.3 %collective-permute-start.5 = (bf16[3,128,4096]{2,1,0:T(8,128)(2,1)}, bf16[3,128,4096]{2,1,0:T(8,128)(2,1)}, u32[]{:S(2)}, u32[]{:S(2)}) collective-permute-start(bf16[3,128,4096]{2,1,0:T(8,128)(2,1)} %collective-permute-done.1.refs_2_), channel_id=1, source_target_pairs={{2,3},{3,2},{4,5},{5,4},{10,11},{11,10},{12,13},{13,12},{18,19},{1... | collective-permute-start | bytes 9437192 | tf_op jit(solution)/shard_map/ppermute | solution.py:1055
  191.6 25.0 %collective-permute-start.6 = (bf16[3,128,4096]{2,1,0:T(8,128)(2,1)}, bf16[3,128,4096]{2,1,0:T(8,128)(2,1)}, u32[]{:S(2)}, u32[]{:S(2)}) collective-permute-start(bf16[3,128,4096]{2,1,0:T(8,128)(2,1)} %collective-permute-done.2.refs_3_), channel_id=1, source_target_pairs={{2,3},{3,2},{4,5},{5,4},{10,11},{11,10},{12,13},{13,12},{18,19},{1... | collective-permute-start | bytes 9437192 | tf_op jit(solution)/shard_map/ppermute | solution.py:1055
  228.9 13.8 %collective-permute-start.19 = (bf16[128,1024]{1,0:T(8,128)(2,1)S(1)}, bf16[128,1024]{1,0:T(8,128)(2,1)S(1)}, u32[]{:S(2)}, u32[]{:S(2)}) collective-permute-start(bf16[128,1024]{1,0:T(8,128)(2,1)S(1)} %get-tuple-element.744), channel_id=1, source_target_pairs={{2,4},{3,5},{10,12},{11,13},{18,20},{19,21}} | collective-permute-start | bytes 786440 | tf_op jit(solution)/shard_map/ppermute | solution.py:1194
  238.8 13.5 %collective-permute-start.17 = (bf16[128,1024]{1,0:T(8,128)(2,1)S(1)}, bf16[128,1024]{1,0:T(8,128)(2,1)S(1)}, u32[]{:S(2)}, u32[]{:S(2)}) collective-permute-start(bf16[128,1024]{1,0:T(8,128)(2,1)S(1)} %get-tuple-element.743), channel_id=1, source_target_pairs={{2,4},{3,5},{10,12},{11,13},{18,20},{19,21}} | collective-permute-start | bytes 786440 | tf_op jit(solution)/shard_map/ppermute | solution.py:1194
  241.4 13.5 %collective-permute-start.23 = (bf16[128,1024]{1,0:T(8,128)(2,1)S(1)}, bf16[128,1024]{1,0:T(8,128)(2,1)S(1)}, u32[]{:S(2)}, u32[]{:S(2)}) collective-permute-start(bf16[128,1024]{1,0:T(8,128)(2,1)S(1)} %get-tuple-element.780), channel_id=1, source_target_pairs={{2,4},{3,5},{10,12},{11,13},{18,20},{19,21}} | collective-permute-start | bytes 786440 | tf_op jit(solution)/shard_map/ppermute | solution.py:1194
  242.7 21.3 %collective-permute-start.21 = (bf16[128,1024]{1,0:T(8,128)(2,1)S(1)}, bf16[128,1024]{1,0:T(8,128)(2,1)S(1)}, u32[]{:S(2)}, u32[]{:S(2)}) collective-permute-start(bf16[128,1024]{1,0:T(8,128)(2,1)S(1)} %get-tuple-element.779), channel_id=1, source_target_pairs={{2,4},{3,5},{10,12},{11,13},{18,20},{19,21}} | collective-permute-start | bytes 786440 | tf_op jit(solution)/shard_map/ppermute | solution.py:1194
  253.7 12.4 %collective-permute-start.27 = (bf16[128,1024]{1,0:T(8,128)(2,1)S(1)}, bf16[128,1024]{1,0:T(8,128)(2,1)S(1)}, u32[]{:S(2)}, u32[]{:S(2)}) collective-permute-start(bf16[128,1024]{1,0:T(8,128)(2,1)S(1)} %get-tuple-element.816), channel_id=1, source_target_pairs={{2,4},{3,5},{10,12},{11,13},{18,20},{19,21}} | collective-permute-start | bytes 786440 | tf_op jit(solution)/shard_map/ppermute | solution.py:1194
  255.0 18.8 %collective-permute-start.25 = (bf16[128,1024]{1,0:T(8,128)(2,1)S(1)}, bf16[128,1024]{1,0:T(8,128)(2,1)S(1)}, u32[]{:S(2)}, u32[]{:S(2)}) collective-permute-start(bf16[128,1024]{1,0:T(8,128)(2,1)S(1)} %get-tuple-element.815), channel_id=1, source_target_pairs={{2,4},{3,5},{10,12},{11,13},{18,20},{19,21}} | collective-permute-start | bytes 786440 | tf_op jit(solution)/shard_map/ppermute | solution.py:1194
  365.3 12.4 %collective-permute-start.53 = (bf16[128,1024]{1,0:T(8,128)(2,1)S(1)}, bf16[128,1024]{1,0:T(8,128)(2,1)S(1)}, u32[]{:S(2)}, u32[]{:S(2)}) collective-permute-start(bf16[128,1024]{1,0:T(8,128)(2,1)S(1)} %get-tuple-element.1171), channel_id=1, source_target_pairs={{4,2},{5,3},{12,10},{13,11},{20,18},{21,19}} | collective-permute-start | bytes 786440 | tf_op jit(solution)/shard_map/ppermute | solution.py:1213
  375.6 12.6 %collective-permute-start.57 = (bf16[128,1024]{1,0:T(8,128)(2,1)S(1)}, bf16[128,1024]{1,0:T(8,128)(2,1)S(1)}, u32[]{:S(2)}, u32[]{:S(2)}) collective-permute-start(bf16[128,1024]{1,0:T(8,128)(2,1)S(1)} %get-tuple-element.1195), channel_id=1, source_target_pairs={{4,2},{5,3},{12,10},{13,11},{20,18},{21,19}} | collective-permute-start | bytes 786440 | tf_op jit(solution)/shard_map/ppermute | solution.py:1213
  386.1 12.4 %collective-permute-start.61 = (bf16[128,1024]{1,0:T(8,128)(2,1)S(1)}, bf16[128,1024]{1,0:T(8,128)(2,1)S(1)}, u32[]{:S(2)}, u32[]{:S(2)}) collective-permute-start(bf16[128,1024]{1,0:T(8,128)(2,1)S(1)} %get-tuple-element.1219), channel_id=1, source_target_pairs={{4,2},{5,3},{12,10},{13,11},{20,18},{21,19}} | collective-permute-start | bytes 786440 | tf_op jit(solution)/shard_map/ppermute | solution.py:1213
  396.4 12.6 %collective-permute-start.65 = (bf16[128,1024]{1,0:T(8,128)(2,1)S(1)}, bf16[128,1024]{1,0:T(8,128)(2,1)S(1)}, u32[]{:S(2)}, u32[]{:S(2)}) collective-permute-start(bf16[128,1024]{1,0:T(8,128)(2,1)S(1)} %get-tuple-element.1243), channel_id=1, source_target_pairs={{4,2},{5,3},{12,10},{13,11},{20,18},{21,19}} | collective-permute-start | bytes 786440 | tf_op jit(solution)/shard_map/ppermute | solution.py:1213
  462.7 17.6 %collective-permute-start.82 = (bf16[4,128,4096]{2,1,0:T(8,128)(2,1)}, bf16[4,128,4096]{2,1,0:T(8,128)(2,1)}, u32[]{:S(2)}, u32[]{:S(2)}) collective-permute-start(bf16[4,128,4096]{2,1,0:T(8,128)(2,1)} %get-tuple-element.1365.refs_3_), channel_id=1, source_target_pairs={{2,3},{3,2},{4,5},{5,4},{10,11},{11,10},{12,13},{13,12},{18,19},{1... | collective-permute-start | bytes 12582920 | tf_op jit(solution)/shard_map/ppermute | solution.py:1055
  465.3 14.9 %collective-permute-start.83 = (bf16[4,512,1024]{2,1,0:T(8,128)(2,1)}, bf16[4,512,1024]{2,1,0:T(8,128)(2,1)}, u32[]{:S(2)}, u32[]{:S(2)}) collective-permute-start(bf16[4,512,1024]{2,1,0:T(8,128)(2,1)} %get-tuple-element.1370), channel_id=1, source_target_pairs={{2,3},{3,2},{4,5},{5,4},{10,11},{11,10},{12,13},{13,12},{18,19},{1... | collective-permute-start | bytes 12582920 | tf_op jit(solution)/shard_map/ppermute | solution.py:1055
  467.9 12.4 %collective-permute-start.84 = (bf16[4,128,4096]{2,1,0:T(8,128)(2,1)}, bf16[4,128,4096]{2,1,0:T(8,128)(2,1)}, u32[]{:S(2)}, u32[]{:S(2)}) collective-permute-start(bf16[4,128,4096]{2,1,0:T(8,128)(2,1)} %get-tuple-element.1371), channel_id=1, source_target_pairs={{2,3},{3,2},{4,5},{5,4},{10,11},{11,10},{12,13},{13,12},{18,19},{1... | collective-permute-start | bytes 12582920 | tf_op jit(solution)/shard_map/ppermute | solution.py:1055
  478.8 13.3 %collective-permute-start.94 = (bf16[272,1024]{1,0:T(8,128)(2,1)S(1)}, bf16[272,1024]{1,0:T(8,128)(2,1)S(1)}, u32[]{:S(2)}, u32[]{:S(2)}) collective-permute-start(bf16[272,1024]{1,0:T(8,128)(2,1)S(1)} %pad_maximum_fusion.4), channel_id=1, source_target_pairs={{2,4},{3,5},{4,2},{5,3},{10,12},{11,13},{12,10},{13,11},{18,20},{1... | collective-permute-start | bytes 1671176 | tf_op jit(solution)/shard_map/ppermute | solution.py:1051
  487.0 539.9 %collective-permute-start.85 = (bf16[3,128,4096]{2,1,0:T(8,128)(2,1)}, bf16[3,128,4096]{2,1,0:T(8,128)(2,1)}, u32[]{:S(2)}, u32[]{:S(2)}) collective-permute-start(bf16[3,128,4096]{2,1,0:T(8,128)(2,1)} %get-tuple-element.1373), channel_id=1, source_target_pairs={{2,0},{3,1},{4,6},{5,7},{10,8},{11,9},{12,14},{13,15},{18,16},{19,... | collective-permute-start | bytes 9437192 | tf_op jit(solution)/shard_map/ppermute | solution.py:1051
  488.4 538.5 %collective-permute-start.86 = (bf16[3,128,4096]{2,1,0:T(8,128)(2,1)}, bf16[3,128,4096]{2,1,0:T(8,128)(2,1)}, u32[]{:S(2)}, u32[]{:S(2)}) collective-permute-start(bf16[3,128,4096]{2,1,0:T(8,128)(2,1)} %get-tuple-element.1374), channel_id=1, source_target_pairs={{2,4},{3,5},{4,2},{5,3},{10,12},{11,13},{12,10},{13,11},{18,20},{1... | collective-permute-start | bytes 9437192 | tf_op jit(solution)/shard_map/ppermute | solution.py:1051
  490.8 536.1 %collective-permute-start.87 = (bf16[3,128,4096]{2,1,0:T(8,128)(2,1)}, bf16[3,128,4096]{2,1,0:T(8,128)(2,1)}, u32[]{:S(2)}, u32[]{:S(2)}) collective-permute-start(bf16[3,128,4096]{2,1,0:T(8,128)(2,1)} %get-tuple-element.1375), channel_id=1, source_target_pairs={{2,6},{3,7},{4,0},{5,1},{10,14},{11,15},{12,8},{13,9},{18,22},{19,... | collective-permute-start | bytes 9437192 | tf_op jit(solution)/shard_map/ppermute | solution.py:1051
  492.3 486.7 %collective-permute-start.95 = (bf16[272,1024]{1,0:T(8,128)(2,1)S(1)}, bf16[272,1024]{1,0:T(8,128)(2,1)S(1)}, u32[]{:S(2)}, u32[]{:S(2)}) collective-permute-start(bf16[272,1024]{1,0:T(8,128)(2,1)S(1)} %fusion.37), channel_id=1, source_target_pairs={{2,0},{3,1},{4,6},{5,7},{10,8},{11,9},{12,14},{13,15},{18,16},{19,... | collective-permute-start | bytes 1671176 | tf_op jit(solution)/shard_map/ppermute | solution.py:1051
  979.4 14.4 %collective-permute-start.96 = (bf16[256,1024]{1,0:T(8,128)(2,1)S(1)}, bf16[256,1024]{1,0:T(8,128)(2,1)S(1)}, u32[]{:S(2)}, u32[]{:S(2)}) collective-permute-start(bf16[256,1024]{1,0:T(8,128)(2,1)S(1)} %slice.332), channel_id=1, source_target_pairs={{0,8},{8,0},{16,24},{24,16},{1,9},{9,1},{17,25},{25,17},{2,10},{10... | collective-permute-start | bytes 1572872 | tf_op jit(solution)/shard_map/ppermute | solution.py:1058
  982.1 11.9 %collective-permute-start.79 = (bf16[1,256,1024]{2,1,0:T(8,128)(2,1)S(1)}, bf16[1,256,1024]{2,1,0:T(8,128)(2,1)S(1)}, u32[]{:S(2)}, u32[]{:S(2)}) collective-permute-start(bf16[1,256,1024]{2,1,0:T(8,128)(2,1)S(1)} %copy-done.40), channel_id=1, source_target_pairs={{4,6},{5,7},{12,14},{13,15},{20,22},{21,23},{28,30},{29,31}} | collective-permute-start | bytes 1572872 | tf_op jit(solution)/shard_map/ppermute | solution.py:1051
  993.8 12.9 %collective-permute-start.97 = (bf16[256,1024]{1,0:T(8,128)(2,1)S(1)}, bf16[256,1024]{1,0:T(8,128)(2,1)S(1)}, u32[]{:S(2)}, u32[]{:S(2)}) collective-permute-start(bf16[256,1024]{1,0:T(8,128)(2,1)S(1)} %slice_add_fusion.1), channel_id=1, source_target_pairs={{0,16},{8,24},{16,0},{24,8},{1,17},{9,25},{17,1},{25,9},{2,18},{10... | collective-permute-start | bytes 1572872 | tf_op jit(solution)/shard_map/ppermute | solution.py:1058
  993.9 17.1 %collective-permute-start.80 = (bf16[1,256,1024]{2,1,0:T(8,128)(2,1)}, bf16[1,256,1024]{2,1,0:T(8,128)(2,1)}, u32[]{:S(2)}, u32[]{:S(2)}) collective-permute-start(bf16[1,256,1024]{2,1,0:T(8,128)(2,1)} %get-tuple-element.1368), channel_id=1, source_target_pairs={{4,2},{5,3},{12,10},{13,11},{20,18},{21,19},{28,26},{29,27}} | collective-permute-start | bytes 1572872 | tf_op jit(solution)/shard_map/ppermute | solution.py:1051
  1007.6 15.1 %collective-permute-start.81 = (bf16[1,256,1024]{2,1,0:T(8,128)(2,1)}, bf16[1,256,1024]{2,1,0:T(8,128)(2,1)}, u32[]{:S(2)}, u32[]{:S(2)}) collective-permute-start(bf16[1,256,1024]{2,1,0:T(8,128)(2,1)} %get-tuple-element.1369), channel_id=1, source_target_pairs={{4,0},{5,1},{12,8},{13,9},{20,16},{21,17},{28,24},{29,25}} | collective-permute-start | bytes 1572872 | tf_op jit(solution)/shard_map/ppermute | solution.py:1051
  1011.1 14.3 %collective-permute-start.98 = (bf16[256,1024]{1,0:T(8,128)(2,1)}, bf16[256,1024]{1,0:T(8,128)(2,1)S(1)}, u32[]{:S(2)}, u32[]{:S(2)}) collective-permute-start(bf16[256,1024]{1,0:T(8,128)(2,1)} %get-tuple-element.1393), channel_id=1, source_target_pairs={{0,1},{1,0},{2,3},{3,2},{4,5},{5,4},{6,7},{7,6},{8,9},{9,8},{10,11... | collective-permute-start | bytes 1572872 | tf_op jit(solution)/shard_map/ppermute | solution.py:1055
  (126 other events, 2251.5 us)
